TPU v7x, 32 devices: a whole 2x2x4 slice. The times are simulated.
32 devices in a mesh: rows: 16 (over z, x, core), lev: 2 (over y).
Axes of the slice: x: 2, y: 2, z: 4, core: 2. Of those that a mesh axis runs over, the one named last changes fastest.
Arguments:
- field: bfloat16 [2, 8, 256, 64, 1024], P(None, 'lev', 'rows'), may hold values from -6 to 6
- spectral_weight: bfloat16 [3, 64, 64, 64, 64], P(None, None, 'rows'), may hold values from -5 to 5
- local_weight: bfloat16 [64, 64], replicated, may hold values from -0.75 to 0.75
- local_bias: float32 [64], replicated, may hold values from -4 to 4
- gate_weight: bfloat16 [64, 256], replicated, may hold values from -0.75 to 0.75
- up_weight: bfloat16 [64, 256], replicated, may hold values from -0.75 to 0.75
- down_weight: bfloat16 [256, 64], replicated, may hold values from -0.375 to 0.375
Outputs:
- updated: bfloat16 [2, 8, 256, 64, 1024], P(None, 'lev', 'rows')
All inputs are finite; a program needn't handle non-finite values.
Results may differ from a plain program's by a relative error of at most 0.02.
Values may be sent and summed in bfloat16 or wider, within the bound.
No kernel may reach another device: no remote copies, remote signals or barrier semaphores. Data moves between devices by JAX's collectives and lax.ppermute only.
A program may use at most 128 MiB of HBM per device.

v0:
```python
import math

import jax
import jax.numpy as jnp
from jax import lax
from jax.sharding import PartitionSpec as P


def extended(cells, sides, width):
    for axis, dim in sides:
        count = lax.axis_size(axis)
        ends = count - 1
        head = lax.slice_in_dim(cells, 0, width, axis=dim)
        tail = lax.slice_in_dim(cells, cells.shape[dim] - width, cells.shape[dim], axis=dim)
        cells = jnp.concatenate(
            [
                lax.ppermute(tail, axis, [(i, (i + 1) % count) for i in range(ends)]),
                cells,
                lax.ppermute(head, axis, [((i + 1) % count, i) for i in range(ends)]),
            ],
            axis=dim,
        )
    return cells


def cas_rows(positions, count, modes):
    freq = jnp.arange(modes, dtype=jnp.int32) - modes // 2
    turns = positions[:, None] * freq[None, :] % count
    angle = 2.0 * math.pi / count * turns.astype(jnp.float32)
    return (jnp.cos(angle) + jnp.sin(angle)) / math.sqrt(count)


def body(field, spectral_weight, local_weight, local_bias, gate_weight, up_weight, down_weight):
    high = lax.Precision.HIGHEST
    batch, levels, lat_rows, chans, lon_cells = field.shape
    ranks = lax.axis_size("rows")
    lat_total = lat_rows * ranks
    lat_modes = spectral_weight.shape[1]
    lon_modes = spectral_weight.shape[2] * ranks
    lon_table = cas_rows(jnp.arange(lon_cells, dtype=jnp.int32), lon_cells, lon_modes).astype(
        jnp.bfloat16
    )
    own_rows = lax.axis_index("rows") * lat_rows + jnp.arange(lat_rows, dtype=jnp.int32)
    along = jnp.dot(field.reshape(-1, lon_cells), lon_table, preferred_element_type=jnp.float32)
    along = along.reshape(batch, levels, lat_rows, chans, lon_modes)
    own_table = cas_rows(own_rows, lat_total, lat_modes)
    partial_modes = jnp.einsum("nk,blncm->blkcm", own_table, along, precision=high)
    modes = lax.psum_scatter(
        partial_modes.astype(jnp.bfloat16), "rows", scatter_dimension=4, tiled=True
    )
    padded = extended(modes, (("lev", 1),), 1)
    mixed = jnp.einsum(
        "kmco,blkcm->blkom",
        spectral_weight[0],
        padded[:, 0:levels],
        preferred_element_type=jnp.float32,
    )
    mixed = mixed + jnp.einsum(
        "kmco,blkcm->blkom",
        spectral_weight[1],
        padded[:, 1 : levels + 1],
        preferred_element_type=jnp.float32,
    )
    mixed = mixed + jnp.einsum(
        "kmco,blkcm->blkom",
        spectral_weight[2],
        padded[:, 2 : levels + 2],
        preferred_element_type=jnp.float32,
    )
    mixed_b = mixed.astype(jnp.bfloat16)
    own_inverse = cas_rows(own_rows, lat_total, lat_modes)
    values = jnp.einsum(
        "nk,blkom->blnom",
        own_inverse,
        lax.all_gather(mixed_b, "rows", axis=4, tiled=True).astype(jnp.float32),
        precision=high,
    )
    back_b = values.astype(jnp.bfloat16)

    def finish(pair):
        grid, coarse = pair
        spectral = jnp.dot(
            coarse.reshape(-1, lon_modes), lon_table.T, preferred_element_type=jnp.float32
        )
        spectral = spectral.reshape(lat_rows, chans, lon_cells)
        local = jnp.einsum("co,ncx->nox", local_weight, grid, preferred_element_type=jnp.float32)
        value = spectral + local + local_bias[None, :, None]
        act = jax.nn.gelu(value, approximate=False).astype(jnp.bfloat16)
        gate = jnp.einsum("ch,ncx->nhx", gate_weight, act, preferred_element_type=jnp.float32)
        upper = jnp.einsum("ch,ncx->nhx", up_weight, act, preferred_element_type=jnp.float32)
        hidden = (jax.nn.silu(gate) * upper).astype(jnp.bfloat16)
        down = jnp.einsum("hc,nhx->ncx", down_weight, hidden, preferred_element_type=jnp.float32)
        return (grid.astype(jnp.float32) + down).astype(jnp.bfloat16)

    result = lax.map(
        finish,
        (
            field.reshape(batch * levels, lat_rows, chans, lon_cells),
            back_b.reshape(batch * levels, lat_rows, chans, lon_modes),
        ),
    )
    return result.reshape(batch, levels, lat_rows, chans, lon_cells)


def solution(mesh):
    return jax.shard_map(
        body,
        mesh=mesh,
        in_specs=(
            P(None, "lev", "rows", None, None),
            P(None, None, "rows", None, None),
            P(),
            P(),
            P(),
            P(),
            P(),
        ),
        out_specs=P(None, "lev", "rows", None, None),
        check_vma=False,
    )
```

profile of v0, /device:TPU:0, one launch (start us, length us, event | category | flops | bytes accessed | tf_op | source)
XLA Modules:
  0.0 625.0 jit_solution(17359710535924696727)
XLA Ops:
  6.5 10.2 %convolution_bitcast_fusion = f32[8192,64]{0,1:T(8,128)S(1)} fusion(bf16[8192,1024]{1,0:T(8,128)(2,1)} %bitcast.134, s32[64]{0:T(128)S(1)} %iota_add_fusion.1), kind=kOutput, calls=%fused_computation.70 | convolution fusion | flops 1074855936 | bytes 18874624 | tf_op jit(solution)/shard_map/dot_general | solution.py:44
  16.7 3.0 reshape.31
  19.8 6.3 %copy.13 = f32[2,4,16,64,64]{4,2,3,1,0:T(8,128)} copy(f32[2,4,16,64,64]{3,2,1,0,4:T(8,128)} %reshape.31) | data formatting | bytes 4194304 | tf_op jit(solution)/shard_map/reshape | solution.py:45
  26.0 29.5 %convert_bitcast_fusion = bf16[2,4,64,64,64]{2,4,3,1,0:T(8,128)(2,1)} fusion(f32[2,4,16,64,64]{4,2,3,1,0:T(8,128)} %copy.13, s32[64]{0:T(128)S(1)} %iota_add_fusion.1, s32[16]{0:T(128)S(1)} %iota_add_fusion), kind=kOutput, calls=%fused_computation.71 | convolution fusion | flops 404766720 | bytes 6291776 | tf_op jit(solution)/shard_map/nk,blncm->blkcm/dot_general | solution.py:47
  55.5 12.8 %copy.14 = bf16[2,4,64,64,64]{3,2,1,0,4:T(8,128)(2,1)} copy(bf16[2,4,64,64,64]{2,4,3,1,0:T(8,128)(2,1)} %convert_bitcast_fusion) | data formatting | bytes 8388608 | tf_op jit(solution)/shard_map/convert_element_type | solution.py:49
  68.4 107.5 %reduce-scatter.2.cloned.1.call-done = bf16[2,4,64,64,4]{3,2,1,0,4:T(8,128)(2,1)} async-done(((bf16[2,4,64,64,64]{3,2,1,0,4:T(8,128)(2,1)}), bf16[2,4,64,64,4]{3,2,1,0,4:T(8,128)(2,1)}) %reduce-scatter.2.cloned.1.call-update) | async-done | bytes 262160 | tf_op jit(solution)/shard_map/reduce_scatter | solution.py:48
  176.9 3.4 collective-permute-start
  181.8 3.6 fusion.56
  185.4 1.9 collective-permute-done.1
  187.4 3.4 fusion.54
  190.8 3.5 fusion.58
  194.3 2.5 fusion.67
  197.0 74.0 %all-gather.2.cloned.1.call-done = bf16[2,4,64,64,64]{3,2,1,0,4:T(8,128)(2,1)} async-done(((bf16[2,4,64,64,4]{3,2,1,0,4:T(8,128)(2,1)}), bf16[2,4,64,64,64]{3,2,1,0,4:T(8,128)(2,1)}) %all-gather.2.cloned.1.call-update) | async-done | bytes 4194320 | tf_op jit(solution)/shard_map/all_gather | solution.py:75
  271.0 12.0 %copy.15 = bf16[2,4,64,64,64]{2,4,3,1,0:T(8,128)(2,1)} copy(bf16[2,4,64,64,64]{3,2,1,0,4:T(8,128)(2,1)} %all-gather.2.cloned.1.call-done) | data formatting | bytes 8388608 | tf_op jit(solution)/shard_map/all_gather | solution.py:75
  283.0 22.1 %convolution_convert_fusion = bf16[2,4,64,64,16]{3,4,2,1,0:T(8,128)(2,1)S(1)} fusion(bf16[2,4,64,64,64]{2,4,3,1,0:T(8,128)(2,1)} %copy.15, s32[64]{0:T(128)S(1)} %iota_add_fusion.1, s32[16]{0:T(128)S(1)} %iota_add_fusion), kind=kOutput, calls=%fused_computation.81 | convolution fusion | flops 403193856 | bytes 5243200 | tf_op jit(solution)/shard_map/nk,blkom->blnom/dot_general | solution.py:72
  305.1 313.0 %while.11 = (s32[]{:T(128)}, bf16[8,16,64,1024]{3,2,1,0:T(8,128)(2,1)}, bf16[8,16,64,1024]{3,2,1,0:T(8,128)(2,1)}, bf16[8,16,64,64]{3,1,2,0:T(8,128)(2,1)S(1)}, ...) while((s32[]{:T(128)}, ...), condition=%wide.region_2.3_spmd.clone, body=%wide.region_1.2_spmd.clone.sunk | while | flops 2060451840 | bytes 78489232 | solution.py:95
  305.4 1.8 fusion.120
  307.2 3.3 fusion.121
  310.4 13.0 %fusion.122 = f32[16,1024,256]{2,1,0:T(8,128)} fusion(bf16[64,256]{1,0:T(8,128)(2,1)S(1)} %get-tuple-element.221, f32[16,64,1024]{2,1,0:T(8,128)S(1)} %get-tuple-element.190, u16[64,1024]{1,0:T(8,128)(2,1)S(1)} %get-tuple-element.191), kind=kOutput, calls=%fused_computation.58.clone.1 | convolution fusion | flops 608174080 | bytes 21135360 | tf_op jit(solution)/shard_map/while/body/eval_jaxpr/ch,ncx->nhx/dot_general | solution.py:90
  323.4 21.0 %fusion.123 = bf16[8,16,64,1024]{3,2,1,0:T(8,128)(2,1)} fusion(bf16[8,16,64,1024]{3,2,1,0:T(8,128)(2,1)} %get-tuple-element.204, s32[]{:T(128)} %get-tuple-element.203, bf16[8,16,64,1024]{3,2,1,0:T(8,128)(2,1)} %get-tuple-element.216, f32[16,1024,256]{2,1,0:T(8,128)} %fusion.122, bf16[256,64]{0,1:T(8,128)(2,1)S(1)} %get-tuple-element.222, ...), kind=kOutput, calls=%fused_computation.34.clone.1 | convolution fusion | flops 1173356544 | bytes 25362944 | tf_op jit(solution)/shard_map/while/body/eval_jaxpr/hc,nhx->ncx/dot_general | solution.py:92
  344.5 1.8 fusion.120
  346.3 3.3 fusion.121
  349.5 13.0 %fusion.122 = f32[16,1024,256]{2,1,0:T(8,128)} fusion(bf16[64,256]{1,0:T(8,128)(2,1)S(1)} %get-tuple-element.221, f32[16,64,1024]{2,1,0:T(8,128)S(1)} %get-tuple-element.190, u16[64,1024]{1,0:T(8,128)(2,1)S(1)} %get-tuple-element.191), kind=kOutput, calls=%fused_computation.58.clone.1 | convolution fusion | flops 608174080 | bytes 21135360 | tf_op jit(solution)/shard_map/while/body/eval_jaxpr/ch,ncx->nhx/dot_general | solution.py:90
  362.5 21.0 %fusion.123 = bf16[8,16,64,1024]{3,2,1,0:T(8,128)(2,1)} fusion(bf16[8,16,64,1024]{3,2,1,0:T(8,128)(2,1)} %get-tuple-element.204, s32[]{:T(128)} %get-tuple-element.203, bf16[8,16,64,1024]{3,2,1,0:T(8,128)(2,1)} %get-tuple-element.216, f32[16,1024,256]{2,1,0:T(8,128)} %fusion.122, bf16[256,64]{0,1:T(8,128)(2,1)S(1)} %get-tuple-element.222, ...), kind=kOutput, calls=%fused_computation.34.clone.1 | convolution fusion | flops 1173356544 | bytes 25362944 | tf_op jit(solution)/shard_map/while/body/eval_jaxpr/hc,nhx->ncx/dot_general | solution.py:92
  383.6 1.8 fusion.120
  385.4 3.3 fusion.121
  388.6 13.0 %fusion.122 = f32[16,1024,256]{2,1,0:T(8,128)} fusion(bf16[64,256]{1,0:T(8,128)(2,1)S(1)} %get-tuple-element.221, f32[16,64,1024]{2,1,0:T(8,128)S(1)} %get-tuple-element.190, u16[64,1024]{1,0:T(8,128)(2,1)S(1)} %get-tuple-element.191), kind=kOutput, calls=%fused_computation.58.clone.1 | convolution fusion | flops 608174080 | bytes 21135360 | tf_op jit(solution)/shard_map/while/body/eval_jaxpr/ch,ncx->nhx/dot_general | solution.py:90
  401.6 21.0 %fusion.123 = bf16[8,16,64,1024]{3,2,1,0:T(8,128)(2,1)} fusion(bf16[8,16,64,1024]{3,2,1,0:T(8,128)(2,1)} %get-tuple-element.204, s32[]{:T(128)} %get-tuple-element.203, bf16[8,16,64,1024]{3,2,1,0:T(8,128)(2,1)} %get-tuple-element.216, f32[16,1024,256]{2,1,0:T(8,128)} %fusion.122, bf16[256,64]{0,1:T(8,128)(2,1)S(1)} %get-tuple-element.222, ...), kind=kOutput, calls=%fused_computation.34.clone.1 | convolution fusion | flops 1173356544 | bytes 25362944 | tf_op jit(solution)/shard_map/while/body/eval_jaxpr/hc,nhx->ncx/dot_general | solution.py:92
  422.7 1.8 fusion.120
  424.5 3.3 fusion.121
  427.7 13.0 %fusion.122 = f32[16,1024,256]{2,1,0:T(8,128)} fusion(bf16[64,256]{1,0:T(8,128)(2,1)S(1)} %get-tuple-element.221, f32[16,64,1024]{2,1,0:T(8,128)S(1)} %get-tuple-element.190, u16[64,1024]{1,0:T(8,128)(2,1)S(1)} %get-tuple-element.191), kind=kOutput, calls=%fused_computation.58.clone.1 | convolution fusion | flops 608174080 | bytes 21135360 | tf_op jit(solution)/shard_map/while/body/eval_jaxpr/ch,ncx->nhx/dot_general | solution.py:90
  440.7 21.0 %fusion.123 = bf16[8,16,64,1024]{3,2,1,0:T(8,128)(2,1)} fusion(bf16[8,16,64,1024]{3,2,1,0:T(8,128)(2,1)} %get-tuple-element.204, s32[]{:T(128)} %get-tuple-element.203, bf16[8,16,64,1024]{3,2,1,0:T(8,128)(2,1)} %get-tuple-element.216, f32[16,1024,256]{2,1,0:T(8,128)} %fusion.122, bf16[256,64]{0,1:T(8,128)(2,1)S(1)} %get-tuple-element.222, ...), kind=kOutput, calls=%fused_computation.34.clone.1 | convolution fusion | flops 1173356544 | bytes 25362944 | tf_op jit(solution)/shard_map/while/body/eval_jaxpr/hc,nhx->ncx/dot_general | solution.py:92
  461.8 1.8 fusion.120
  463.6 3.3 fusion.121
  466.8 13.0 %fusion.122 = f32[16,1024,256]{2,1,0:T(8,128)} fusion(bf16[64,256]{1,0:T(8,128)(2,1)S(1)} %get-tuple-element.221, f32[16,64,1024]{2,1,0:T(8,128)S(1)} %get-tuple-element.190, u16[64,1024]{1,0:T(8,128)(2,1)S(1)} %get-tuple-element.191), kind=kOutput, calls=%fused_computation.58.clone.1 | convolution fusion | flops 608174080 | bytes 21135360 | tf_op jit(solution)/shard_map/while/body/eval_jaxpr/ch,ncx->nhx/dot_general | solution.py:90
  479.8 21.0 %fusion.123 = bf16[8,16,64,1024]{3,2,1,0:T(8,128)(2,1)} fusion(bf16[8,16,64,1024]{3,2,1,0:T(8,128)(2,1)} %get-tuple-element.204, s32[]{:T(128)} %get-tuple-element.203, bf16[8,16,64,1024]{3,2,1,0:T(8,128)(2,1)} %get-tuple-element.216, f32[16,1024,256]{2,1,0:T(8,128)} %fusion.122, bf16[256,64]{0,1:T(8,128)(2,1)S(1)} %get-tuple-element.222, ...), kind=kOutput, calls=%fused_computation.34.clone.1 | convolution fusion | flops 1173356544 | bytes 25362944 | tf_op jit(solution)/shard_map/while/body/eval_jaxpr/hc,nhx->ncx/dot_general | solution.py:92
  500.9 1.8 fusion.120
  502.7 3.3 fusion.121
  505.9 13.0 %fusion.122 = f32[16,1024,256]{2,1,0:T(8,128)} fusion(bf16[64,256]{1,0:T(8,128)(2,1)S(1)} %get-tuple-element.221, f32[16,64,1024]{2,1,0:T(8,128)S(1)} %get-tuple-element.190, u16[64,1024]{1,0:T(8,128)(2,1)S(1)} %get-tuple-element.191), kind=kOutput, calls=%fused_computation.58.clone.1 | convolution fusion | flops 608174080 | bytes 21135360 | tf_op jit(solution)/shard_map/while/body/eval_jaxpr/ch,ncx->nhx/dot_general | solution.py:90
  518.9 21.0 %fusion.123 = bf16[8,16,64,1024]{3,2,1,0:T(8,128)(2,1)} fusion(bf16[8,16,64,1024]{3,2,1,0:T(8,128)(2,1)} %get-tuple-element.204, s32[]{:T(128)} %get-tuple-element.203, bf16[8,16,64,1024]{3,2,1,0:T(8,128)(2,1)} %get-tuple-element.216, f32[16,1024,256]{2,1,0:T(8,128)} %fusion.122, bf16[256,64]{0,1:T(8,128)(2,1)S(1)} %get-tuple-element.222, ...), kind=kOutput, calls=%fused_computation.34.clone.1 | convolution fusion | flops 1173356544 | bytes 25362944 | tf_op jit(solution)/shard_map/while/body/eval_jaxpr/hc,nhx->ncx/dot_general | solution.py:92
  540.0 1.8 fusion.120
  541.8 3.3 fusion.121
  545.0 13.0 %fusion.122 = f32[16,1024,256]{2,1,0:T(8,128)} fusion(bf16[64,256]{1,0:T(8,128)(2,1)S(1)} %get-tuple-element.221, f32[16,64,1024]{2,1,0:T(8,128)S(1)} %get-tuple-element.190, u16[64,1024]{1,0:T(8,128)(2,1)S(1)} %get-tuple-element.191), kind=kOutput, calls=%fused_computation.58.clone.1 | convolution fusion | flops 608174080 | bytes 21135360 | tf_op jit(solution)/shard_map/while/body/eval_jaxpr/ch,ncx->nhx/dot_general | solution.py:90
  558.0 21.0 %fusion.123 = bf16[8,16,64,1024]{3,2,1,0:T(8,128)(2,1)} fusion(bf16[8,16,64,1024]{3,2,1,0:T(8,128)(2,1)} %get-tuple-element.204, s32[]{:T(128)} %get-tuple-element.203, bf16[8,16,64,1024]{3,2,1,0:T(8,128)(2,1)} %get-tuple-element.216, f32[16,1024,256]{2,1,0:T(8,128)} %fusion.122, bf16[256,64]{0,1:T(8,128)(2,1)S(1)} %get-tuple-element.222, ...), kind=kOutput, calls=%fused_computation.34.clone.1 | convolution fusion | flops 1173356544 | bytes 25362944 | tf_op jit(solution)/shard_map/while/body/eval_jaxpr/hc,nhx->ncx/dot_general | solution.py:92
  579.1 1.8 fusion.120
  580.9 3.3 fusion.121
  584.1 13.0 %fusion.122 = f32[16,1024,256]{2,1,0:T(8,128)} fusion(bf16[64,256]{1,0:T(8,128)(2,1)S(1)} %get-tuple-element.221, f32[16,64,1024]{2,1,0:T(8,128)S(1)} %get-tuple-element.190, u16[64,1024]{1,0:T(8,128)(2,1)S(1)} %get-tuple-element.191), kind=kOutput, calls=%fused_computation.58.clone.1 | convolution fusion | flops 608174080 | bytes 21135360 | tf_op jit(solution)/shard_map/while/body/eval_jaxpr/ch,ncx->nhx/dot_general | solution.py:90
  597.1 21.0 %fusion.123 = bf16[8,16,64,1024]{3,2,1,0:T(8,128)(2,1)} fusion(bf16[8,16,64,1024]{3,2,1,0:T(8,128)(2,1)} %get-tuple-element.204, s32[]{:T(128)} %get-tuple-element.203, bf16[8,16,64,1024]{3,2,1,0:T(8,128)(2,1)} %get-tuple-element.216, f32[16,1024,256]{2,1,0:T(8,128)} %fusion.122, bf16[256,64]{0,1:T(8,128)(2,1)S(1)} %get-tuple-element.222, ...), kind=kOutput, calls=%fused_computation.34.clone.1 | convolution fusion | flops 1173356544 | bytes 25362944 | tf_op jit(solution)/shard_map/while/body/eval_jaxpr/hc,nhx->ncx/dot_general | solution.py:92
  (48 shorter events, 3.1 us)
Async XLA Ops:
  6.5 169.3 %reduce-scatter.2.cloned.1.call-start = ((), (), s32[]{:S(2)}) async-start(), calls=%async_computation.1 | async-start | bytes 8912896 | tf_op jit(solution)/shard_map/reduce_scatter | solution.py:48
  68.3 202.7 %all-gather.2.cloned.1.call-start = ((), (), s32[]{:S(2)}) async-start(), calls=%async_computation.2 | async-start | bytes 8912896 | tf_op jit(solution)/shard_map/all_gather | solution.py:75
  175.9 11.3 %copy-start.1 = (bf16[2,4,64,64,4]{3,2,1,0,4:T(8,128)(2,1)S(1)}, bf16[2,4,64,64,4]{3,2,1,0,4:T(8,128)(2,1)}, u32[]{:S(2)}) copy-start(bf16[2,4,64,64,4]{3,2,1,0,4:T(8,128)(2,1)} %reduce-scatter.2.cloned.1.call-done) | copy-start | bytes 786436
  176.9 8.4 %collective-permute-start = (bf16[2,1,64,64,4]{3,2,1,0,4:T(8,128)(2,1)S(1)}, bf16[2,1,64,64,4]{3,2,1,0,4:T(8,128)(2,1)S(1)}, u32[]{:S(2)}, u32[]{:S(2)}) collective-permute-start(bf16[2,1,64,64,4]{3,2,1,0,4:T(8,128)(2,1)S(1)} %get-tuple-element.125), channel_id=1, source_target_pairs={{0,1},{2,3},{4,5},{6,7},{8,9},{10,11},{12,13},{14,15},{16,17},{18,... | collective-permute-start | bytes 196616 | tf_op jit(solution)/shard_map/ppermute | solution.py:17
  180.3 6.9 %collective-permute-start.1 = (bf16[2,1,64,64,4]{3,2,1,0,4:T(8,128)(2,1)S(1)}, bf16[2,1,64,64,4]{3,2,1,0,4:T(8,128)(2,1)S(1)}, u32[]{:S(2)}, u32[]{:S(2)}) collective-permute-start(bf16[2,1,64,64,4]{3,2,1,0,4:T(8,128)(2,1)S(1)} %get-tuple-element.126), channel_id=1, source_target_pairs={{1,0},{3,2},{5,4},{7,6},{9,8},{11,10},{13,12},{15,14},{17,16},{19,... | collective-permute-start | bytes 196616 | tf_op jit(solution)/shard_map/ppermute | solution.py:19
  190.8 6.0 copy-start.2
  283.0 22.1 %copy-start.3 = (f32[64]{0:T(128)S(1)}, f32[64]{0:T(128)}, u32[]{:S(2)}) copy-start(f32[64]{0:T(128)} %param.12) | copy-start | bytes 772
  283.0 22.1 %copy-start.4 = (bf16[64,256]{1,0:T(8,128)(2,1)S(1)}, bf16[64,256]{1,0:T(8,128)(2,1)}, u32[]{:S(2)}) copy-start(bf16[64,256]{1,0:T(8,128)(2,1)} %param.13) | copy-start | bytes 98308
  283.0 22.1 %copy-start.5 = (bf16[64,256]{1,0:T(8,128)(2,1)S(1)}, bf16[64,256]{1,0:T(8,128)(2,1)}, u32[]{:S(2)}) copy-start(bf16[64,256]{1,0:T(8,128)(2,1)} %param.14) | copy-start | bytes 98308
  283.0 22.1 %copy-start.6 = (bf16[256,64]{0,1:T(8,128)(2,1)S(1)}, bf16[256,64]{0,1:T(8,128)(2,1)}, u32[]{:S(2)}) copy-start(bf16[256,64]{0,1:T(8,128)(2,1)} %param.15) | copy-start | bytes 98308
  310.4 13.0 %copy-start = (f32[16,64,1024]{2,1,0:T(8,128)}, f32[16,64,1024]{2,1,0:T(8,128)S(1)}, u32[]{:S(2)}) copy-start(f32[16,64,1024]{2,1,0:T(8,128)S(1)} %get-tuple-element.190) | copy-start | bytes 12582916 | tf_op jit(solution)/shard_map/while
  349.5 13.0 %copy-start = (f32[16,64,1024]{2,1,0:T(8,128)}, f32[16,64,1024]{2,1,0:T(8,128)S(1)}, u32[]{:S(2)}) copy-start(f32[16,64,1024]{2,1,0:T(8,128)S(1)} %get-tuple-element.190) | copy-start | bytes 12582916 | tf_op jit(solution)/shard_map/while
  388.6 13.0 %copy-start = (f32[16,64,1024]{2,1,0:T(8,128)}, f32[16,64,1024]{2,1,0:T(8,128)S(1)}, u32[]{:S(2)}) copy-start(f32[16,64,1024]{2,1,0:T(8,128)S(1)} %get-tuple-element.190) | copy-start | bytes 12582916 | tf_op jit(solution)/shard_map/while
  427.7 13.0 %copy-start = (f32[16,64,1024]{2,1,0:T(8,128)}, f32[16,64,1024]{2,1,0:T(8,128)S(1)}, u32[]{:S(2)}) copy-start(f32[16,64,1024]{2,1,0:T(8,128)S(1)} %get-tuple-element.190) | copy-start | bytes 12582916 | tf_op jit(solution)/shard_map/while
  466.8 13.0 %copy-start = (f32[16,64,1024]{2,1,0:T(8,128)}, f32[16,64,1024]{2,1,0:T(8,128)S(1)}, u32[]{:S(2)}) copy-start(f32[16,64,1024]{2,1,0:T(8,128)S(1)} %get-tuple-element.190) | copy-start | bytes 12582916 | tf_op jit(solution)/shard_map/while
  505.9 13.0 %copy-start = (f32[16,64,1024]{2,1,0:T(8,128)}, f32[16,64,1024]{2,1,0:T(8,128)S(1)}, u32[]{:S(2)}) copy-start(f32[16,64,1024]{2,1,0:T(8,128)S(1)} %get-tuple-element.190) | copy-start | bytes 12582916 | tf_op jit(solution)/shard_map/while
  545.0 13.0 %copy-start = (f32[16,64,1024]{2,1,0:T(8,128)}, f32[16,64,1024]{2,1,0:T(8,128)S(1)}, u32[]{:S(2)}) copy-start(f32[16,64,1024]{2,1,0:T(8,128)S(1)} %get-tuple-element.190) | copy-start | bytes 12582916 | tf_op jit(solution)/shard_map/while
  584.1 13.0 %copy-start = (f32[16,64,1024]{2,1,0:T(8,128)}, f32[16,64,1024]{2,1,0:T(8,128)S(1)}, u32[]{:S(2)}) copy-start(f32[16,64,1024]{2,1,0:T(8,128)S(1)} %get-tuple-element.190) | copy-start | bytes 12582916 | tf_op jit(solution)/shard_map/while
Sparse Core Ops, SparseCore 0:
  68.4 107.4 reduce-scatter.1
  197.0 73.9 all-gather.1
where the time goes:
time: 626 us; the launch traced here: 625 us
  matrix products  385 us (62%)
  waiting for transfers between devices  183 us (29%)
  local copies, waits for them, and re-layouts  35.4 us (6%)
  between operations  13.5 us (2%)
    dot_general x8, matrix products, finish(): jnp.einsum('hc,nhx->ncx', down_weight, hidden, preferred_element_type=jnp...  168 us
    reduce_scatter x1, waiting for transfers between devices, body(): lax.psum_scatter(partial_modes.astype(jnp.bfloat16), 'rows', scatter_dime...  108 us
    dot_general x8, matrix products, finish(): jnp.einsum('ch,ncx->nhx', up_weight, act, preferred_element_type=jnp.floa...  104 us
    all_gather x1, waiting for transfers between devices, body(): lax.all_gather(mixed_b, 'rows', axis=4, tiled=True).astype(jnp.float32)  74 us
    dot_general x1, matrix products, body(): jnp.einsum('nk,blncm->blkcm', own_table, along, precision=high)  29.5 us
    dot_general x8, matrix products, finish(): jnp.einsum('co,ncx->nox', local_weight, grid, preferred_element_type=jnp....  26 us
    dot_general x1, matrix products, body(): jnp.einsum('nk,blkom->blnom', own_inverse, lax.all_gather(mixed_b, 'rows'...  22.1 us
    dot_general x8, matrix products, finish(): jnp.dot(coarse.reshape(-1, lon_modes), lon_table.T, preferred_element_typ...  14.2 us
  transfers between devices with their start and end apart: 4, of which 3 were waited for; matrix products, arithmetic and copies ran while one was open for 1% of the time, Pallas kernels for 0%

commit v1 on v0

v1 whole, which is shorter than its diff:
```python
import functools
import math

import jax
import jax.numpy as jnp
import ml_dtypes
import numpy as np
from jax import lax
from jax.experimental import pallas as pl
from jax.experimental.pallas import tpu as pltpu
from jax.sharding import PartitionSpec as P

BF = jnp.bfloat16
F32 = jnp.float32
NT = (((1,), (1,)), ((), ()))


def cas_table(count, modes):
    turns = np.arange(count)[:, None] * (np.arange(modes)[None, :] - modes // 2) % count
    angle = 2.0 * math.pi / count * turns
    return ((np.cos(angle) + np.sin(angle)) / math.sqrt(count)).astype(np.float32)


def split(table):
    high = table.astype(ml_dtypes.bfloat16)
    low = (table - high.astype(np.float32)).astype(ml_dtypes.bfloat16)
    return high, low


def call(kernel, grid, in_specs, out_specs, out_shape, scratch, flops, moved, **kw):
    return pl.pallas_call(
        kernel,
        grid=grid,
        in_specs=in_specs,
        out_specs=out_specs,
        out_shape=out_shape,
        scratch_shapes=scratch,
        compiler_params=pltpu.CompilerParams(
            dimension_semantics=("arbitrary",) * len(grid), vmem_limit_bytes=48 * 2**20
        ),
        cost_estimate=pl.CostEstimate(flops=flops, bytes_accessed=moved, transcendentals=0),
        **kw,
    )


def lanes(rows, wide):
    return pltpu.VMEM((wide // 128, rows, 128), F32)


def every(ref, start, size, stride):
    return jnp.concatenate(
        [ref[p, pl.ds(start, size, stride=stride), :] for p in range(ref.shape[0])], axis=1
    )


def put(ref, at, value):
    for p in range(ref.shape[0]):
        ref[p, at, :] = value[:, p * 128 : (p + 1) * 128]


def whole(shape):
    return pl.BlockSpec(shape, lambda *_: (0,) * len(shape))


def forward_kernel(ranks, field_ref, lon_ref, out_ref, held):
    _, _, rows, chans, cells = field_ref.shape
    modes = lon_ref.shape[0]
    band = modes // ranks
    values = lax.dot_general(
        lon_ref[...], field_ref[0, 0].reshape(rows * chans, cells), NT, preferred_element_type=F32
    )
    for n in range(rows):
        piece = values[:, n * chans : (n + 1) * chans]
        row = jnp.concatenate([piece[j * ranks : (j + 1) * ranks] for j in range(band)], axis=1)
        put(held, pl.ds(n * ranks, ranks), row)
    for r in range(ranks):
        out_ref[r, 0] = every(held, r, rows, ranks).astype(BF)


def forward(field, lon_rows, batch_at, ranks):
    _, levels, rows, chans, cells = field.shape
    modes = lon_rows.shape[0]
    wide = modes // ranks * chans
    return call(
        functools.partial(forward_kernel, ranks),
        (levels,),
        [
            pl.BlockSpec((1, 1, rows, chans, cells), lambda l: (batch_at, l, 0, 0, 0)),
            whole((modes, cells)),
        ],
        pl.BlockSpec((ranks, 1, rows, wide), lambda l: (0, l, 0, 0)),
        jax.ShapeDtypeStruct((ranks, levels, rows, wide), BF),
        [lanes(rows * ranks, wide)],
        2 * levels * rows * chans * cells * modes,
        levels * rows * chans * cells * 2,
    )(field, lon_rows)


def modes_kernel(table_ref, along_ref, out_ref):
    ranks, levels, rows, wide = along_ref.shape
    count = out_ref.shape[1]
    for l in range(levels):
        both = jnp.dot(
            table_ref[...],
            along_ref[:, l].reshape(ranks * rows, wide),
            preferred_element_type=F32,
        )
        out_ref[l] = (both[:count] + both[count:]).astype(BF)


def to_modes(table, along):
    ranks, levels, rows, wide = along.shape
    count = table.shape[0] // 2
    return call(
        modes_kernel,
        (1,),
        [whole(table.shape), whole(along.shape)],
        whole((levels, count, wide)),
        jax.ShapeDtypeStruct((levels, count, wide), BF),
        [],
        2 * levels * 2 * count * ranks * rows * wide,
        along.size * 2,
    )(table, along)


def mix_kernel(
    levels, below_ref, modes_ref, above_ref, weight_ref, table_ref, out_ref, held, mixed
):
    lat_modes, band, chans = weight_ref.shape[1:4]
    ranks, _, rows, wide = out_ref.shape
    step = held.shape[1] // lat_modes

    for l in range(levels + 2):
        source = below_ref[0] if l == 0 else above_ref[0] if l > levels else modes_ref[l - 1]
        put(held, pl.ds(l, lat_modes, stride=step), source.astype(F32))

    def one(k, carry):
        at = pl.multiple_of(k * step, 8)
        tile = jnp.concatenate([held[p, pl.ds(at, step), :] for p in range(wide // 128)], axis=1)
        parts = []
        for j in range(band):
            lhs = jnp.concatenate(
                [tile[d : d + levels, j * chans : (j + 1) * chans] for d in range(3)], axis=1
            ).astype(BF)
            weight = weight_ref[:, k, j].reshape(3 * chans, chans)
            parts.append(jnp.dot(lhs, weight, preferred_element_type=F32))
        put(mixed, pl.ds(at, levels), jnp.concatenate(parts, axis=1))
        return carry

    lax.fori_loop(0, lat_modes, one, 0, unroll=4)
    for l in range(levels):
        value = every(mixed, l, lat_modes, step).astype(BF)
        back = jnp.dot(
            table_ref[...], jnp.concatenate([value, value], axis=0), preferred_element_type=F32
        )
        out_ref[:, l] = back.astype(BF).reshape(ranks, rows, wide)


def mix(below, modes, above, weight, table, ranks):
    levels, lat_modes, wide = modes.shape
    rows = table.shape[0] // ranks
    step = (levels + 2 + 7) // 8 * 8
    return call(
        functools.partial(mix_kernel, levels),
        (1,),
        [
            whole(below.shape),
            whole(modes.shape),
            whole(above.shape),
            whole(weight.shape),
            whole(table.shape),
        ],
        whole((ranks, levels, rows, wide)),
        jax.ShapeDtypeStruct((ranks, levels, rows, wide), BF),
        [lanes(lat_modes * step, wide), lanes(lat_modes * step, wide)],
        weight.size * 2 * levels,
        weight.size * 4,
    )(below, modes, above, weight, table)


def gelu(value):
    return 0.5 * value * (1.0 + lax.erf(value * math.sqrt(0.5)))


def finish_kernel(
    block, field_ref, back_ref, lon_ref, local_ref, bias_ref, into_ref, down_ref, *rest
):
    out_ref, held, coarse = rest[-3:]
    ranks, _, rows, wide = back_ref.shape
    chans, cells = field_ref.shape[3:]
    band = wide // chans
    hid = down_ref.shape[1]
    at = pl.program_id(1)

    @pl.when(at == 0)
    def _():
        put(held, slice(None), back_ref[:, 0].astype(F32).reshape(ranks * rows, wide))
        for n in range(rows):
            tile = every(held, n, ranks, rows)
            stacked = jnp.concatenate(
                [tile[:, j * chans : (j + 1) * chans] for j in range(band)], axis=0
            )
            coarse[n] = jnp.concatenate([stacked.T.astype(BF), local_ref[...]], axis=1)

    tile_x = min(256, cells)

    def one(i, carry):
        n = at * block + i
        lhs = coarse[n]
        for x in range(0, cells, tile_x):
            span = slice(x, x + tile_x)
            grid = field_ref[0, 0, i, :, span]
            value = jnp.dot(
                lhs,
                jnp.concatenate([lon_ref[:, span], grid], axis=0),
                preferred_element_type=F32,
            )
            act = gelu(value + bias_ref[...]).astype(BF)
            both = jnp.dot(into_ref[...], act, preferred_element_type=F32)
            half = both[:hid]
            hidden = ((half + half * jnp.tanh(half)) * both[hid:]).astype(BF)
            down = jnp.dot(down_ref[...], hidden, preferred_element_type=F32)
            out_ref[0, 0, i, :, span] = (grid.astype(F32) + down).astype(BF)
        return carry

    lax.fori_loop(0, block, one, 0)


def finish(field, back, lon_rows, local, bias, into, down, batch_at, earlier, block=4):
    batch, levels, rows, chans, cells = field.shape
    ranks, _, _, wide = back.shape
    modes = lon_rows.shape[0]
    block = math.gcd(block, rows)
    spot = pl.BlockSpec((1, 1, block, chans, cells), lambda l, n: (batch_at, l, n, 0, 0))
    operands = [field, back, lon_rows, local, bias, into, down]
    in_specs = [
        spot,
        pl.BlockSpec((ranks, 1, rows, wide), lambda l, n: (0, l, 0, 0)),
        whole(lon_rows.shape),
        whole(local.shape),
        whole(bias.shape),
        whole(into.shape),
        whole(down.shape),
    ]
    kw = {}
    if earlier is not None:
        operands.append(earlier)
        in_specs.append(pl.BlockSpec(memory_space=pl.ANY))
        kw["input_output_aliases"] = {7: 0}
    return call(
        functools.partial(finish_kernel, block),
        (levels, rows // block),
        in_specs,
        spot,
        jax.ShapeDtypeStruct(field.shape, BF),
        [
            lanes(ranks * rows, wide),
            pltpu.VMEM((rows, chans, modes + chans), BF),
        ],
        2 * levels * rows * cells * chans * (modes + chans + 3 * down.shape[1]),
        levels * rows * chans * cells * 4,
        **kw,
    )(*operands)


def body(field, spectral_weight, local_weight, local_bias, gate_weight, up_weight, down_weight):
    batch, levels, rows, chans, cells = field.shape
    ranks = lax.axis_size("rows")
    sides = lax.axis_size("lev")
    lat_modes = spectral_weight.shape[1]
    band = spectral_weight.shape[2]
    lon_modes = band * ranks
    lon_rows = cas_table(cells, lon_modes).astype(ml_dtypes.bfloat16).T
    lon_rows = lon_rows.reshape(ranks, band, cells).swapaxes(0, 1).reshape(lon_modes, cells)
    lon_rows = jnp.asarray(np.ascontiguousarray(lon_rows))
    high, low = split(cas_table(rows * ranks, lat_modes))
    gather_table = jnp.asarray(np.concatenate([high.T, low.T], axis=0))
    spread_table = jnp.asarray(np.concatenate([high, low], axis=1))

    into = jnp.concatenate([gate_weight * BF(0.5), up_weight], axis=1).T
    down = down_weight.T
    local = local_weight.T
    bias = jnp.broadcast_to(local_bias[:, None], (chans, min(256, cells)))

    backs = []
    for b in range(batch):
        along = forward(field, lon_rows, b, ranks)
        along = lax.all_to_all(along, "rows", 0, 0, tiled=True)
        modes = to_modes(gather_table, along)
        below = lax.ppermute(modes[levels - 1 :], "lev", [(i, i + 1) for i in range(sides - 1)])
        above = lax.ppermute(modes[:1], "lev", [(i + 1, i) for i in range(sides - 1)])
        back = mix(below, modes, above, spectral_weight, spread_table, ranks)
        backs.append(lax.all_to_all(back, "rows", 0, 0, tiled=True))
    result = None
    for b in range(batch):
        result = finish(field, backs[b], lon_rows, local, bias, into, down, b, result)
    return result


def solution(mesh):
    return jax.shard_map(
        body,
        mesh=mesh,
        in_specs=(
            P(None, "lev", "rows", None, None),
            P(None, None, "rows", None, None),
            P(),
            P(),
            P(),
            P(),
            P(),
        ),
        out_specs=P(None, "lev", "rows", None, None),
        check_vma=False,
    )
```

time: 626 us -> 276 us (0.44)
  matrix products: 385 us -> 0 us
  Pallas kernels: 0 us -> 227 us
  waiting for transfers between devices: 183 us -> 10.5 us
  local copies, waits for them, and re-layouts: 35.4 us -> 1.35 us
  starting transfers between devices: 4.88 us -> 35.1 us
  between operations: 13.5 us -> 0.22 us
    dot_general x38 -> x0, matrix products: 385 us -> none  [the longest x8 168 us: finish(): jnp.einsum('hc,nhx->ncx', down_weight, hidden, preferred_element_type=jnp...]
    pallas_call x0 -> x8, Pallas kernels: none -> 227 us  [the longest x2 188 us: finish(): call(functools.partial(finish_kernel, block), (levels, rows // block), in...]
    reduce_scatter x1 -> x0, waiting for transfers between devices: 108 us -> none  [body(): lax.psum_scatter(partial_modes.astype(jnp.bfloat16), 'rows', scatter_dime...]
    all_gather x1 -> x0, waiting for transfers between devices: 74 us -> none  [body(): lax.all_gather(mixed_b, 'rows', axis=4, tiled=True).astype(jnp.float32)]
    all_to_all x0 -> x4, starting transfers between devices: none -> 23.5 us  [the longest x2 12 us: body(): backs.append(lax.all_to_all(back, 'rows', 0, 0, tiled=True))]
    convert_element_type x1 -> x0, local copies, waits for them, and re-layouts: 12.8 us -> none  [body(): partial_modes.astype(jnp.bfloat16)]
    all_gather x1 -> x0, local copies, waits for them, and re-layouts: 12 us -> none  [body(): lax.all_gather(mixed_b, 'rows', axis=4, tiled=True).astype(jnp.float32)]
    reshape x2 -> x0, local copies, waits for them, and re-layouts: 9.29 us -> none  [body(): along = along.reshape(batch, levels, lat_rows, chans, lon_modes)]
  transfers between devices with their start and end apart: 4 -> 8, of which waited for: 3 -> 3; matrix products, arithmetic and copies ran while one was open for 1% -> 0% of each run, Pallas kernels for 0% -> 46%
where the time goes in v1:
time: 276 us; the launch traced here: 275 us
  Pallas kernels  227 us (82%)
  starting transfers between devices  35.1 us (13%)
  waiting for transfers between devices  10.5 us (4%)
    pallas_call x2, Pallas kernels, finish(): call(functools.partial(finish_kernel, block), (levels, rows // block), in...  188 us
    pallas_call x2, Pallas kernels, mix(): call(functools.partial(mix_kernel, levels), (1,), [whole(below.shape), wh...  25.5 us
    pallas_call x2, Pallas kernels, forward(): call(functools.partial(forward_kernel, ranks), (levels,), [pl.BlockSpec((...  13.5 us
    all_to_all x2, starting transfers between devices, body(): backs.append(lax.all_to_all(back, 'rows', 0, 0, tiled=True))  12 us
    all_to_all x2, starting transfers between devices, body(): along = lax.all_to_all(along, 'rows', 0, 0, tiled=True)  11.5 us
    ppermute x2, starting transfers between devices, body(): lax.ppermute(modes[levels - 1:], 'lev', [(i, i + 1) for i in range(sides...  9.09 us
    all_to_all x2, waiting for transfers between devices, body(): along = lax.all_to_all(along, 'rows', 0, 0, tiled=True)  7.68 us
  transfers between devices with their start and end apart: 8, of which 3 were waited for; matrix products, arithmetic and copies ran while one was open for 0% of the time, Pallas kernels for 46%

profile of v1, /device:TPU:0, one launch (start us, length us, event | category | flops | bytes accessed | tf_op | source)
XLA Modules:
  0.0 274.6 jit_solution(7476722974270763121)
XLA Ops:
  0.0 0.0 copy-start
  0.0 0.9 copy-done
  0.9 0.0 copy-start.1
  0.9 0.0 copy-start.3
  0.9 0.0 copy-start.2
  0.9 6.8 %shard_map.103 = bf16[16,4,16,256]{3,2,1,0:T(8,128)(2,1)} custom-call(bf16[2,4,16,64,1024]{4,3,2,1,0:T(8,128)(2,1)} %field_ref.7, bf16[64,1024]{1,0:T(8,128)(2,1)S(1)} %copy-done), custom_call_target="tpu_custom_call" | custom-call | flops 536870912 | bytes 8388608 | tf_op jit(solution)/shard_map/pallas_call | solution.py:84
  7.7 7.4 %all-to-all-start.2 = ((bf16[16,4,16,256]{3,2,1,0:T(8,128)(2,1)}), bf16[16,4,16,256]{3,2,1,0:T(8,128)(2,1)S(1)}, u32[]{:S(2)}, u32[]{:S(2)}) async-start(bf16[16,4,16,256]{3,2,1,0:T(8,128)(2,1)} %shard_map.103), calls=%async_computation.2 | async-start | bytes 1048576 | tf_op jit(solution)/shard_map/all_to_all | solution.py:288
  15.1 0.0 copy-done.1
  15.1 0.0 copy-start.7
  15.1 0.0 copy-start.5
  15.1 0.0 copy-start.6
  15.1 6.7 %shard_map.100 = bf16[16,4,16,256]{3,2,1,0:T(8,128)(2,1)} custom-call(bf16[2,4,16,64,1024]{4,3,2,1,0:T(8,128)(2,1)} %field_ref.7, bf16[64,1024]{1,0:T(8,128)(2,1)S(1)} %copy-done.1), custom_call_target="tpu_custom_call" | custom-call | flops 536870912 | bytes 8388608 | tf_op jit(solution)/shard_map/pallas_call | solution.py:84
  21.9 0.0 copy-start.8
  21.9 0.0 copy-start.4
  21.9 7.7 %all-to-all-done.2.along_ref = bf16[16,4,16,256]{3,2,1,0:T(8,128)(2,1)S(1)} async-done(((bf16[16,4,16,256]{3,2,1,0:T(8,128)(2,1)}), bf16[16,4,16,256]{3,2,1,0:T(8,128)(2,1)S(1)}, u32[]{:S(2)}, u32[]{:S(2)}) %all-to-all-start.2) | async-done | bytes 524320 | tf_op jit(solution)/shard_map/all_to_all | solution.py:288
  29.5 4.1 %all-to-all-start = ((bf16[16,4,16,256]{3,2,1,0:T(8,128)(2,1)}), bf16[16,4,16,256]{3,2,1,0:T(8,128)(2,1)S(1)}, u32[]{:S(2)}, u32[]{:S(2)}) async-start(bf16[16,4,16,256]{3,2,1,0:T(8,128)(2,1)} %shard_map.100), calls=%async_computation | async-start | bytes 1048576 | tf_op jit(solution)/shard_map/all_to_all | solution.py:288
  33.7 0.0 copy-done.3
  33.7 0.2 shard_map.104.modes_ref
  33.9 1.3 collective-permute-start.3
  35.2 4.5 %collective-permute-start.2 = (bf16[1,64,256]{2,1,0:T(8,128)(2,1)S(1)}, bf16[1,64,256]{2,1,0:T(8,128)(2,1)S(1)}, u32[]{:S(2)}, u32[]{:S(2)}) collective-permute-start(bf16[1,64,256]{2,1,0:T(8,128)(2,1)S(1)} %get-tuple-element.6), channel_id=1, source_target_pairs={{0,1},{2,3},{4,5},{6,7},{8,9},{10,11},{12,13},{14,15},{16,17},{18,... | collective-permute-start | bytes 98312 | tf_op jit(solution)/shard_map/ppermute | solution.py:290
  39.8 0.0 collective-permute-done.3.above_ref
  39.8 1.6 collective-permute-done.2.below_ref
  41.3 0.0 copy-done.2
  41.3 12.7 %shard_map.105 = bf16[16,4,16,256]{3,2,1,0:T(8,128)(2,1)} custom-call(bf16[1,64,256]{2,1,0:T(8,128)(2,1)S(1)} %collective-permute-done.2.below_ref, bf16[4,64,256]{2,1,0:T(8,128)(2,1)S(1)} %shard_map.104.modes_ref, bf16[1,64,256]{2,1,0:T(8,128)(2,1)S(1)} %collective-permute-done.3.above_ref, bf16[3,64,4,64,64]{4,3,2,1,0:T(8,128)(2,1)} %weight_ref.3, ...), custom_call_target="tpu_custom_call" | custom-call | flops 25165824 | bytes 12582912 | tf_op jit(solution)/shard_map/pallas_call | solution.py:163
  54.1 0.0 all-to-all-done.along_ref
  54.1 6.0 %all-to-all-start.3 = ((bf16[16,4,16,256]{3,2,1,0:T(8,128)(2,1)}), bf16[16,4,16,256]{3,2,1,0:T(8,128)(2,1)S(1)}, u32[]{:S(2)}, u32[]{:S(2)}) async-start(bf16[16,4,16,256]{3,2,1,0:T(8,128)(2,1)} %shard_map.105), calls=%async_computation.3 | async-start | bytes 1048576 | tf_op jit(solution)/shard_map/all_to_all | solution.py:293
  60.1 0.2 shard_map.101.modes_ref
  60.3 1.3 collective-permute-start.1
  61.6 4.5 %collective-permute-start = (bf16[1,64,256]{2,1,0:T(8,128)(2,1)S(1)}, bf16[1,64,256]{2,1,0:T(8,128)(2,1)S(1)}, u32[]{:S(2)}, u32[]{:S(2)}) collective-permute-start(bf16[1,64,256]{2,1,0:T(8,128)(2,1)S(1)} %get-tuple-element.8), channel_id=1, source_target_pairs={{0,1},{2,3},{4,5},{6,7},{8,9},{10,11},{12,13},{14,15},{16,17},{18,... | collective-permute-start | bytes 98312 | tf_op jit(solution)/shard_map/ppermute | solution.py:290
  66.2 0.0 copy-done.7
  66.2 0.1 copy.15
  66.3 0.0 copy-done.5
  66.3 0.1 copy.16
  66.4 0.0 copy-done.6
  66.4 0.1 copy.18
  66.6 0.0 collective-permute-done.1.above_ref
  66.6 1.2 collective-permute-done.below_ref
  67.8 12.7 %shard_map.102 = bf16[16,4,16,256]{3,2,1,0:T(8,128)(2,1)} custom-call(bf16[1,64,256]{2,1,0:T(8,128)(2,1)S(1)} %collective-permute-done.below_ref, bf16[4,64,256]{2,1,0:T(8,128)(2,1)S(1)} %shard_map.101.modes_ref, bf16[1,64,256]{2,1,0:T(8,128)(2,1)S(1)} %collective-permute-done.1.above_ref, bf16[3,64,4,64,64]{4,3,2,1,0:T(8,128)(2,1)} %weight_ref.3, ...), custom_call_target="tpu_custom_call" | custom-call | flops 25165824 | bytes 12582912 | tf_op jit(solution)/shard_map/pallas_call | solution.py:163
  80.5 0.0 all-to-all-done.3.back_ref
  80.5 6.0 %all-to-all-start.1 = ((bf16[16,4,16,256]{3,2,1,0:T(8,128)(2,1)}), bf16[16,4,16,256]{3,2,1,0:T(8,128)(2,1)S(1)}, u32[]{:S(2)}, u32[]{:S(2)}) async-start(bf16[16,4,16,256]{3,2,1,0:T(8,128)(2,1)} %shard_map.102), calls=%async_computation.1 | async-start | bytes 1048576 | tf_op jit(solution)/shard_map/all_to_all | solution.py:293
  86.6 0.0 copy-done.8
  86.6 0.1 broadcast_in_dim.2.bias_ref
  86.7 0.0 copy-done.4
  86.7 94.0 %shard_map.106.rest_0_ = bf16[2,4,16,64,1024]{4,3,2,1,0:T(8,128)(2,1)} custom-call(bf16[2,4,16,64,1024]{4,3,2,1,0:T(8,128)(2,1)} %field_ref.7, bf16[16,4,16,256]{3,2,1,0:T(8,128)(2,1)S(1)} %all-to-all-done.3.back_ref, bf16[64,1024]{1,0:T(8,128)(2,1)S(1)} %copy-done.1, bf16[64,64]{1,0:T(8,128)(2,1)S(1)} %bitcast.4, f32[64,256]{1,0:T(8,128)S(1)} %broadcast_in_dim.2.bias_ref, ...), custom_call_target="tpu_custom_call" | custom-call | flops 7516192768 | bytes 16777216 | tf_op jit(solution)/shard_map/pallas_call | solution.py:250
  180.7 0.0 all-to-all-done.1.back_ref
  180.7 94.0 %shard_map.107 = bf16[2,4,16,64,1024]{4,3,2,1,0:T(8,128)(2,1)} custom-call(bf16[2,4,16,64,1024]{4,3,2,1,0:T(8,128)(2,1)} %field_ref.7, bf16[16,4,16,256]{3,2,1,0:T(8,128)(2,1)S(1)} %all-to-all-done.1.back_ref, bf16[64,1024]{1,0:T(8,128)(2,1)S(1)} %copy-done.1, bf16[64,64]{1,0:T(8,128)(2,1)S(1)} %bitcast.5, ...), custom_call_target="tpu_custom_call", output_to_operand_aliasing={{}: (7, {})} | custom-call | flops 7516192768 | bytes 16777216 | tf_op jit(solution)/shard_map/pallas_call | solution.py:250
  (4 shorter events, 0.1 us)
Async XLA Ops:
  0.0 0.9 copy-start
  0.9 14.2 %copy-start.1 = (bf16[64,1024]{1,0:T(8,128)(2,1)S(1)}, bf16[64,1024]{1,0:T(8,128)(2,1)}, u32[]{:S(2)}) copy-start(bf16[64,1024]{1,0:T(8,128)(2,1)} %constant.8.clone.lon_ref) | copy-start | bytes 393220
  0.9 32.7 %copy-start.3 = (bf16[128,256]{1,0:T(8,128)(2,1)S(1)}, bf16[128,256]{1,0:T(8,128)(2,1)}, u32[]{:S(2)}) copy-start(bf16[128,256]{1,0:T(8,128)(2,1)} %constant.9.clone.table_ref) | copy-start | bytes 196612
  0.9 40.4 %copy-start.2 = (bf16[256,128]{1,0:T(8,128)(2,1)S(1)}, bf16[256,128]{1,0:T(8,128)(2,1)}, u32[]{:S(2)}) copy-start(bf16[256,128]{1,0:T(8,128)(2,1)} %constant.10.clone.table_ref) | copy-start | bytes 196612
  7.7 21.8 %all-to-all-start.2 = ((bf16[16,4,16,256]{3,2,1,0:T(8,128)(2,1)}), bf16[16,4,16,256]{3,2,1,0:T(8,128)(2,1)S(1)}, u32[]{:S(2)}, u32[]{:S(2)}) async-start(bf16[16,4,16,256]{3,2,1,0:T(8,128)(2,1)} %shard_map.103), calls=%async_computation.2 | async-start | bytes 1048576 | tf_op jit(solution)/shard_map/all_to_all | solution.py:288
  15.1 51.1 %copy-start.7 = (bf16[64,64]{1,0:T(8,128)(2,1)S(1)}, bf16[64,64]{1,0:T(8,128)(2,1)}, u32[]{:S(2)}) copy-start(bf16[64,64]{1,0:T(8,128)(2,1)} %param.12) | copy-start | bytes 24580
  15.1 51.2 %copy-start.5 = (bf16[64,256]{1,0:T(8,128)(2,1)S(1)}, bf16[64,256]{1,0:T(8,128)(2,1)}, u32[]{:S(2)}) copy-start(bf16[64,256]{1,0:T(8,128)(2,1)} %param.14) | copy-start | bytes 98308
  15.1 51.3 %copy-start.6 = (bf16[64,256]{1,0:T(8,128)(2,1)S(1)}, bf16[64,256]{1,0:T(8,128)(2,1)}, u32[]{:S(2)}) copy-start(bf16[64,256]{1,0:T(8,128)(2,1)} %param.15) | copy-start | bytes 98308
  21.9 64.7 %copy-start.8 = (f32[64]{0:T(128)S(1)}, f32[64]{0:T(128)}, u32[]{:S(2)}) copy-start(f32[64]{0:T(128)} %param.13) | copy-start | bytes 772
  21.9 64.8 %copy-start.4 = (bf16[256,64]{0,1:T(8,128)(2,1)S(1)}, bf16[256,64]{0,1:T(8,128)(2,1)}, u32[]{:S(2)}) copy-start(bf16[256,64]{0,1:T(8,128)(2,1)} %param.16) | copy-start | bytes 98308
  29.5 24.5 %all-to-all-start = ((bf16[16,4,16,256]{3,2,1,0:T(8,128)(2,1)}), bf16[16,4,16,256]{3,2,1,0:T(8,128)(2,1)S(1)}, u32[]{:S(2)}, u32[]{:S(2)}) async-start(bf16[16,4,16,256]{3,2,1,0:T(8,128)(2,1)} %shard_map.100), calls=%async_computation | async-start | bytes 1048576 | tf_op jit(solution)/shard_map/all_to_all | solution.py:288
  33.9 5.9 %collective-permute-start.3 = (bf16[1,64,256]{2,1,0:T(8,128)(2,1)S(1)}, bf16[1,64,256]{2,1,0:T(8,128)(2,1)S(1)}, u32[]{:S(2)}, u32[]{:S(2)}) collective-permute-start(bf16[1,64,256]{2,1,0:T(8,128)(2,1)S(1)} %get-tuple-element.5), channel_id=1, source_target_pairs={{1,0},{3,2},{5,4},{7,6},{9,8},{11,10},{13,12},{15,14},{17,16},{19,... | collective-permute-start | bytes 98312 | tf_op jit(solution)/shard_map/ppermute | solution.py:291
  35.2 6.1 %collective-permute-start.2 = (bf16[1,64,256]{2,1,0:T(8,128)(2,1)S(1)}, bf16[1,64,256]{2,1,0:T(8,128)(2,1)S(1)}, u32[]{:S(2)}, u32[]{:S(2)}) collective-permute-start(bf16[1,64,256]{2,1,0:T(8,128)(2,1)S(1)} %get-tuple-element.6), channel_id=1, source_target_pairs={{0,1},{2,3},{4,5},{6,7},{8,9},{10,11},{12,13},{14,15},{16,17},{18,... | collective-permute-start | bytes 98312 | tf_op jit(solution)/shard_map/ppermute | solution.py:290
  54.1 26.4 %all-to-all-start.3 = ((bf16[16,4,16,256]{3,2,1,0:T(8,128)(2,1)}), bf16[16,4,16,256]{3,2,1,0:T(8,128)(2,1)S(1)}, u32[]{:S(2)}, u32[]{:S(2)}) async-start(bf16[16,4,16,256]{3,2,1,0:T(8,128)(2,1)} %shard_map.105), calls=%async_computation.3 | async-start | bytes 1048576 | tf_op jit(solution)/shard_map/all_to_all | solution.py:293
  60.3 6.2 %collective-permute-start.1 = (bf16[1,64,256]{2,1,0:T(8,128)(2,1)S(1)}, bf16[1,64,256]{2,1,0:T(8,128)(2,1)S(1)}, u32[]{:S(2)}, u32[]{:S(2)}) collective-permute-start(bf16[1,64,256]{2,1,0:T(8,128)(2,1)S(1)} %get-tuple-element.7), channel_id=1, source_target_pairs={{1,0},{3,2},{5,4},{7,6},{9,8},{11,10},{13,12},{15,14},{17,16},{19,... | collective-permute-start | bytes 98312 | tf_op jit(solution)/shard_map/ppermute | solution.py:291
  61.6 6.1 %collective-permute-start = (bf16[1,64,256]{2,1,0:T(8,128)(2,1)S(1)}, bf16[1,64,256]{2,1,0:T(8,128)(2,1)S(1)}, u32[]{:S(2)}, u32[]{:S(2)}) collective-permute-start(bf16[1,64,256]{2,1,0:T(8,128)(2,1)S(1)} %get-tuple-element.8), channel_id=1, source_target_pairs={{0,1},{2,3},{4,5},{6,7},{8,9},{10,11},{12,13},{14,15},{16,17},{18,... | collective-permute-start | bytes 98312 | tf_op jit(solution)/shard_map/ppermute | solution.py:290
  80.5 100.1 %all-to-all-start.1 = ((bf16[16,4,16,256]{3,2,1,0:T(8,128)(2,1)}), bf16[16,4,16,256]{3,2,1,0:T(8,128)(2,1)S(1)}, u32[]{:S(2)}, u32[]{:S(2)}) async-start(bf16[16,4,16,256]{3,2,1,0:T(8,128)(2,1)} %shard_map.102), calls=%async_computation.1 | async-start | bytes 1048576 | tf_op jit(solution)/shard_map/all_to_all | solution.py:293

commit v2 on v1

--- a/solution.py
+++ b/solution.py
@@ -123,33 +123,58 @@
     )(table, along)
 
 
-def mix_kernel(
-    levels, below_ref, modes_ref, above_ref, weight_ref, table_ref, out_ref, held, mixed
-):
-    lat_modes, band, chans = weight_ref.shape[1:4]
-    ranks, _, rows, wide = out_ref.shape
-    step = held.shape[1] // lat_modes
-
-    for l in range(levels + 2):
-        source = below_ref[0] if l == 0 else above_ref[0] if l > levels else modes_ref[l - 1]
-        put(held, pl.ds(l, lat_modes, stride=step), source.astype(F32))
-
-    def one(k, carry):
-        at = pl.multiple_of(k * step, 8)
-        tile = jnp.concatenate([held[p, pl.ds(at, step), :] for p in range(wide // 128)], axis=1)
-        parts = []
-        for j in range(band):
-            lhs = jnp.concatenate(
-                [tile[d : d + levels, j * chans : (j + 1) * chans] for d in range(3)], axis=1
-            ).astype(BF)
-            weight = weight_ref[:, k, j].reshape(3 * chans, chans)
-            parts.append(jnp.dot(lhs, weight, preferred_element_type=F32))
-        put(mixed, pl.ds(at, levels), jnp.concatenate(parts, axis=1))
-        return carry
-
-    lax.fori_loop(0, lat_modes, one, 0, unroll=4)
+def arrange_kernel(weight_ref, out_ref):
+    shifts, part, band, chans, _ = weight_ref.shape
+    for k in range(part):
+        for d in range(shifts):
+            out_ref[k, d * chans : (d + 1) * chans, :] = jnp.concatenate(
+                [weight_ref[d, k, j] for j in range(band)], axis=1
+            )
+
+
+def arrange(weight, part=8):
+    shifts, lat_modes, band, chans, outs = weight.shape
+    return call(
+        arrange_kernel,
+        (lat_modes // part,),
+        [pl.BlockSpec((shifts, part, band, chans, outs), lambda k: (0, k, 0, 0, 0))],
+        pl.BlockSpec((part, shifts * chans, band * outs), lambda k: (k, 0, 0)),
+        jax.ShapeDtypeStruct((lat_modes, shifts * chans, band * outs), BF),
+        [],
+        weight.size,
+        weight.size * 6,
+    )(weight)
+
+
+def mix_kernel(below_ref, modes_ref, above_ref, weight_ref, table_ref, out_ref, held, mixed):
+    lat_modes, deep, wide = weight_ref.shape
+    ranks, levels, rows, _ = out_ref.shape
+    chans = deep // 3
+    band = wide // chans
+    step = mixed.shape[1] // lat_modes
+
+    near = [below_ref[0].astype(F32)]
+    near += [modes_ref[l].astype(F32) for l in range(levels)]
+    near += [above_ref[0].astype(F32)]
+    fill = [jnp.zeros((lat_modes, held.shape[0] * 128 - deep), F32)]
+    for j in range(band):
+        span = slice(j * chans, (j + 1) * chans)
+        for l in range(levels):
+            row = jnp.concatenate([near[l + d][:, span] for d in range(3)] + fill, axis=1)
+            put(held, pl.ds(j * levels + l, lat_modes, stride=step), row)
+
+    for k in range(lat_modes):
+        at = slice(k * step, (k + 1) * step)
+        lhs = jnp.concatenate([held[p, at, :] for p in range(held.shape[0])], axis=1)
+        lhs = lhs[:, :deep].astype(BF)
+        put(mixed, at, jnp.dot(lhs, weight_ref[k], preferred_element_type=F32))
+
+    owner = lax.broadcasted_iota(jnp.int32, (lat_modes, wide), 1) // chans
     for l in range(levels):
-        value = every(mixed, l, lat_modes, step).astype(BF)
+        value = every(mixed, l, lat_modes, step)
+        for j in range(1, band):
+            value = jnp.where(owner == j, every(mixed, j * levels + l, lat_modes, step), value)
+        value = value.astype(BF)
         back = jnp.dot(
             table_ref[...], jnp.concatenate([value, value], axis=0), preferred_element_type=F32
         )
@@ -159,9 +184,10 @@
 def mix(below, modes, above, weight, table, ranks):
     levels, lat_modes, wide = modes.shape
     rows = table.shape[0] // ranks
-    step = (levels + 2 + 7) // 8 * 8
-    return call(
-        functools.partial(mix_kernel, levels),
+    deep = weight.shape[1]
+    step = (levels * wide * 3 // deep + 7) // 8 * 8
+    return call(
+        mix_kernel,
         (1,),
         [
             whole(below.shape),
@@ -172,70 +198,75 @@
         ],
         whole((ranks, levels, rows, wide)),
         jax.ShapeDtypeStruct((ranks, levels, rows, wide), BF),
-        [lanes(lat_modes * step, wide), lanes(lat_modes * step, wide)],
+        [lanes(lat_modes * step, (deep + 127) // 128 * 128), lanes(lat_modes * step, wide)],
         weight.size * 2 * levels,
-        weight.size * 4,
+        weight.size * 2,
     )(below, modes, above, weight, table)
 
 
-def gelu(value):
-    return 0.5 * value * (1.0 + lax.erf(value * math.sqrt(0.5)))
-
-
 def finish_kernel(
-    block, field_ref, back_ref, lon_ref, local_ref, bias_ref, into_ref, down_ref, *rest
+    ahead, field_ref, back_ref, lon_ref, local_ref, bias_ref, into_ref, down_ref, *rest
 ):
-    out_ref, held, coarse = rest[-3:]
+    out_ref, held, coarse, act, hidden = rest[-5:]
     ranks, _, rows, wide = back_ref.shape
     chans, cells = field_ref.shape[3:]
     band = wide // chans
     hid = down_ref.shape[1]
-    at = pl.program_id(1)
-
-    @pl.when(at == 0)
-    def _():
-        put(held, slice(None), back_ref[:, 0].astype(F32).reshape(ranks * rows, wide))
-        for n in range(rows):
-            tile = every(held, n, ranks, rows)
-            stacked = jnp.concatenate(
-                [tile[:, j * chans : (j + 1) * chans] for j in range(band)], axis=0
-            )
-            coarse[n] = jnp.concatenate([stacked.T.astype(BF), local_ref[...]], axis=1)
-
-    tile_x = min(256, cells)
-
-    def one(i, carry):
-        n = at * block + i
-        lhs = coarse[n]
-        for x in range(0, cells, tile_x):
-            span = slice(x, x + tile_x)
-            grid = field_ref[0, 0, i, :, span]
-            value = jnp.dot(
-                lhs,
-                jnp.concatenate([lon_ref[:, span], grid], axis=0),
-                preferred_element_type=F32,
-            )
-            act = gelu(value + bias_ref[...]).astype(BF)
-            both = jnp.dot(into_ref[...], act, preferred_element_type=F32)
-            half = both[:hid]
-            hidden = ((half + half * jnp.tanh(half)) * both[hid:]).astype(BF)
-            down = jnp.dot(down_ref[...], hidden, preferred_element_type=F32)
-            out_ref[0, 0, i, :, span] = (grid.astype(F32) + down).astype(BF)
+    tile = min(256, cells)
+    spans = [slice(x, x + tile) for x in range(0, cells, tile)]
+
+    put(held, slice(None), back_ref[:, 0].astype(F32).reshape(ranks * rows, wide))
+    for n in range(rows):
+        piece = every(held, n, ranks, rows)
+        stacked = jnp.concatenate(
+            [piece[:, j * chans : (j + 1) * chans] for j in range(band)], axis=0
+        )
+        coarse[n] = jnp.concatenate([stacked.T.astype(BF), local_ref[...]], axis=1)
+
+    def first(n, span):
+        cells_in = jnp.concatenate([lon_ref[:, span], field_ref[0, 0, n, :, span]], axis=0)
+        return jnp.dot(coarse[n], cells_in, preferred_element_type=F32)
+
+    def store_act(u, span, value):
+        value = value + bias_ref[...]
+        half = 0.5 * value
+        act[u, :, span] = (half + half * lax.erf(value * math.sqrt(0.5))).astype(BF)
+
+    def last(u, n, span):
+        down = jnp.dot(down_ref[...], hidden[u, :, span], preferred_element_type=F32)
+        out_ref[0, 0, n, :, span] = (field_ref[0, 0, n, :, span].astype(F32) + down).astype(BF)
+
+    for u in range(ahead):
+        for span in spans:
+            store_act(u, span, first(u, span))
+
+    def one(t, carry):
+        for u in range(ahead):
+            n = t * ahead + u
+            for span in spans:
+                both = jnp.dot(into_ref[...], act[u, :, span], preferred_element_type=F32)
+                last(u, jnp.maximum(n - ahead, 0), span)
+                value = first(jnp.minimum(n + ahead, rows - 1), span)
+                half = both[:hid]
+                hidden[u, :, span] = ((half + half * jnp.tanh(half)) * both[hid:]).astype(BF)
+                store_act(u, span, value)
         return carry
 
-    lax.fori_loop(0, block, one, 0)
-
-
-def finish(field, back, lon_rows, local, bias, into, down, batch_at, earlier, block=4):
+    lax.fori_loop(0, rows // ahead, one, 0)
+    for u in range(ahead):
+        for span in spans:
+            last(u, rows - ahead + u, span)
+
+
+def finish(field, back, lon_rows, local, bias, into, down, batch_at, earlier, ahead=2):
     batch, levels, rows, chans, cells = field.shape
     ranks, _, _, wide = back.shape
     modes = lon_rows.shape[0]
-    block = math.gcd(block, rows)
-    spot = pl.BlockSpec((1, 1, block, chans, cells), lambda l, n: (batch_at, l, n, 0, 0))
+    spot = pl.BlockSpec((1, 1, rows, chans, cells), lambda l: (batch_at, l, 0, 0, 0))
     operands = [field, back, lon_rows, local, bias, into, down]
     in_specs = [
         spot,
-        pl.BlockSpec((ranks, 1, rows, wide), lambda l, n: (0, l, 0, 0)),
+        pl.BlockSpec((ranks, 1, rows, wide), lambda l: (0, l, 0, 0)),
         whole(lon_rows.shape),
         whole(local.shape),
         whole(bias.shape),
@@ -248,19 +279,34 @@
         in_specs.append(pl.BlockSpec(memory_space=pl.ANY))
         kw["input_output_aliases"] = {7: 0}
     return call(
-        functools.partial(finish_kernel, block),
-        (levels, rows // block),
+        functools.partial(finish_kernel, ahead),
+        (levels,),
         in_specs,
         spot,
         jax.ShapeDtypeStruct(field.shape, BF),
         [
             lanes(ranks * rows, wide),
             pltpu.VMEM((rows, chans, modes + chans), BF),
+            pltpu.VMEM((ahead, chans, cells), BF),
+            pltpu.VMEM((ahead, down.shape[1], cells), BF),
         ],
         2 * levels * rows * cells * chans * (modes + chans + 3 * down.shape[1]),
         levels * rows * chans * cells * 4,
         **kw,
     )(*operands)
+
+
+def neighbours(modes, sides):
+    if sides == 2:
+        lower = lax.axis_index("lev") == 0
+        got = lax.ppermute(
+            jnp.where(lower, modes[-1:], modes[:1]), "lev", [(0, 1), (1, 0)]
+        )
+        none = jnp.zeros_like(got)
+        return jnp.where(lower, none, got), jnp.where(lower, got, none)
+    below = lax.ppermute(modes[-1:], "lev", [(i, i + 1) for i in range(sides - 1)])
+    above = lax.ppermute(modes[:1], "lev", [(i + 1, i) for i in range(sides - 1)])
+    return below, above
 
 
 def body(field, spectral_weight, local_weight, local_bias, gate_weight, up_weight, down_weight):
@@ -282,14 +328,18 @@
     local = local_weight.T
     bias = jnp.broadcast_to(local_bias[:, None], (chans, min(256, cells)))
 
+    weight = arrange(spectral_weight)
+    sent = [forward(field, lon_rows, b, ranks) for b in range(batch)]
     backs = []
     for b in range(batch):
-        along = forward(field, lon_rows, b, ranks)
-        along = lax.all_to_all(along, "rows", 0, 0, tiled=True)
+        along = lax.all_to_all(sent[b], "rows", 0, 0, tiled=True)
+        if b == 0:
+            along, weight = lax.optimization_barrier((along, weight))
         modes = to_modes(gather_table, along)
-        below = lax.ppermute(modes[levels - 1 :], "lev", [(i, i + 1) for i in range(sides - 1)])
-        above = lax.ppermute(modes[:1], "lev", [(i + 1, i) for i in range(sides - 1)])
-        back = mix(below, modes, above, spectral_weight, spread_table, ranks)
+        if b + 1 < batch:
+            modes, sent[b + 1] = lax.optimization_barrier((modes, sent[b + 1]))
+        below, above = neighbours(modes, sides)
+        back = mix(below, modes, above, weight, spread_table, ranks)
         backs.append(lax.all_to_all(back, "rows", 0, 0, tiled=True))
     result = None
     for b in range(batch):

time: 276 us -> 143 us (0.52)
  Pallas kernels: 227 us -> 101 us
  starting transfers between devices: 35.1 us -> 24.7 us
  waiting for transfers between devices: 10.5 us -> 15.1 us
    pallas_call x4 -> x5, Pallas kernels: 213 us -> 87.2 us  [the longest x2 67.1 us: finish(): call(functools.partial(finish_kernel, ahead), (levels,), in_specs, spot,...]
    ppermute x4 -> x2, starting transfers between devices: 11.7 us -> 3.17 us  [neighbours(): lax.ppermute(jnp.where(lower, modes[-1:], modes[:1]), 'lev', [(0, 1), (1,...]
    all_to_all x2, waiting for transfers between devices: 0.01 us -> 5.22 us  [body(): backs.append(lax.all_to_all(back, 'rows', 0, 0, tiled=True))]
    all_to_all x2, starting transfers between devices: 12 us -> 8.2 us  [body(): backs.append(lax.all_to_all(back, 'rows', 0, 0, tiled=True))]
  transfers between devices with their start and end apart: 8 -> 6, of which waited for: 3 -> 4; matrix products, arithmetic and copies ran while one was open for 0% -> 0% of each run, Pallas kernels for 46% -> 43%
where the time goes in v2:
time: 143 us
  Pallas kernels  101 us (71%)
  starting transfers between devices  24.7 us (17%)
  waiting for transfers between devices  15.1 us (11%)
    pallas_call x2, Pallas kernels, finish(): call(functools.partial(finish_kernel, ahead), (levels,), in_specs, spot,...  67.1 us
    pallas_call x2, Pallas kernels, forward(): call(functools.partial(forward_kernel, ranks), (levels,), [pl.BlockSpec((...  13.6 us
    all_to_all x2, starting transfers between devices, body(): along = lax.all_to_all(sent[b], 'rows', 0, 0, tiled=True)  13.4 us
    pallas_call x2, Pallas kernels, mix(): call(mix_kernel, (1,), [whole(below.shape), whole(modes.shape), whole(abo...  10 us
    pallas_call x1, Pallas kernels, arrange(): call(arrange_kernel, (lat_modes // part,), [pl.BlockSpec((shifts, part, b...  10 us
    all_to_all x2, starting transfers between devices, body(): backs.append(lax.all_to_all(back, 'rows', 0, 0, tiled=True))  8.2 us
    all_to_all x2, waiting for transfers between devices, body(): along = lax.all_to_all(sent[b], 'rows', 0, 0, tiled=True)  5.44 us
    all_to_all x2, waiting for transfers between devices, body(): backs.append(lax.all_to_all(back, 'rows', 0, 0, tiled=True))  5.22 us
  transfers between devices with their start and end apart: 6, of which 4 were waited for; matrix products, arithmetic and copies ran while one was open for 0% of the time, Pallas kernels for 43%

profile of v2, /device:TPU:0, one launch (start us, length us, event | category | flops | bytes accessed | tf_op | source)
XLA Modules:
  0.0 142.6 jit_solution(16765623833835531283)
XLA Ops:
  0.0 0.0 copy-start
  0.0 0.9 copy-done
  0.9 0.0 copy-start.1
  0.9 6.8 %shard_map.100 = bf16[16,4,16,256]{3,2,1,0:T(8,128)(2,1)} custom-call(bf16[2,4,16,64,1024]{4,3,2,1,0:T(8,128)(2,1)} %field_ref.7, bf16[64,1024]{1,0:T(8,128)(2,1)S(1)} %copy-done), custom_call_target="tpu_custom_call" | custom-call | flops 536870912 | bytes 8388608 | tf_op jit(solution)/shard_map/pallas_call | solution.py:84
  7.7 7.4 %all-to-all-start = ((bf16[16,4,16,256]{3,2,1,0:T(8,128)(2,1)}), bf16[16,4,16,256]{3,2,1,0:T(8,128)(2,1)S(1)}, u32[]{:S(2)}, u32[]{:S(2)}) async-start(bf16[16,4,16,256]{3,2,1,0:T(8,128)(2,1)} %shard_map.100), calls=%async_computation | async-start | bytes 1048576 | tf_op jit(solution)/shard_map/all_to_all | solution.py:335
  15.1 0.0 copy-start.3
  15.1 0.0 copy-start.2
  15.1 10.0 %shard_map.101.weight_ref = bf16[64,192,256]{2,1,0:T(8,128)(2,1)} custom-call(bf16[3,64,4,64,64]{4,3,2,1,0:T(8,128)(2,1)} %weight_ref.1), custom_call_target="tpu_custom_call" | custom-call | flops 3145728 | bytes 18874368 | tf_op jit(solution)/shard_map/pallas_call | solution.py:137
  25.1 0.0 copy-done.1
  25.1 0.0 copy-start.7
  25.1 0.0 copy-start.5
  25.1 0.0 copy-start.6
  25.1 0.0 copy-start.8
  25.1 0.0 copy-start.4
  25.1 6.8 %shard_map.103 = bf16[16,4,16,256]{3,2,1,0:T(8,128)(2,1)} custom-call(bf16[2,4,16,64,1024]{4,3,2,1,0:T(8,128)(2,1)} %field_ref.7, bf16[64,1024]{1,0:T(8,128)(2,1)S(1)} %copy-done.1), custom_call_target="tpu_custom_call" | custom-call | flops 536870912 | bytes 8388608 | tf_op jit(solution)/shard_map/pallas_call | solution.py:84
  31.9 0.0 all-to-all-done.along_ref
  31.9 0.0 copy-done.3
  31.9 0.2 shard_map.102.modes_ref
  32.2 6.0 %all-to-all-start.1 = ((bf16[16,4,16,256]{3,2,1,0:T(8,128)(2,1)}), bf16[16,4,16,256]{3,2,1,0:T(8,128)(2,1)S(1)}, u32[]{:S(2)}, u32[]{:S(2)}) async-start(bf16[16,4,16,256]{3,2,1,0:T(8,128)(2,1)} %shard_map.103), calls=%async_computation.1 | async-start | bytes 1048576 | tf_op jit(solution)/shard_map/all_to_all | solution.py:335
  38.2 1.6 %collective-permute-start.1 = (bf16[1,64,256]{2,1,0:T(8,128)(2,1)S(1)}, bf16[1,64,256]{2,1,0:T(8,128)(2,1)S(1)}, u32[]{:S(2)}, u32[]{:S(2)}) collective-permute-start(bf16[1,64,256]{2,1,0:T(8,128)(2,1)S(1)} %slice_select_fusion.1), channel_id=1, source_target_pairs={{0,1},{1,0},{2,3},{3,2},{4,5},{5,4},{6,7},{7,6},{8,9},{9,8},{10,11... | collective-permute-start | bytes 98312 | tf_op jit(solution)/shard_map/ppermute | solution.py:302
  39.8 2.4 %collective-permute-done.1 = bf16[1,64,256]{2,1,0:T(8,128)(2,1)S(1)} collective-permute-done((bf16[1,64,256]{2,1,0:T(8,128)(2,1)S(1)}, bf16[1,64,256]{2,1,0:T(8,128)(2,1)S(1)}, u32[]{:S(2)}, u32[]{:S(2)}) %collective-permute-start.1) | collective-permute-done | bytes 32800 | tf_op jit(solution)/shard_map/ppermute | solution.py:302
  42.2 0.0 copy-done.2
  42.2 5.0 %shard_map.106 = bf16[16,4,16,256]{3,2,1,0:T(8,128)(2,1)} custom-call(bf16[1,64,256]{2,1,0:T(8,128)(2,1)S(1)} %get-tuple-element.14.below_ref, bf16[4,64,256]{2,1,0:T(8,128)(2,1)S(1)} %shard_map.102.modes_ref, bf16[1,64,256]{2,1,0:T(8,128)(2,1)S(1)} %get-tuple-element.13.above_ref, bf16[64,192,256]{2,1,0:T(8,128)(2,1)} %shard_map.101.weight_ref, ...), custom_call_target="tpu_custom_call" | custom-call | flops 25165824 | bytes 6291456 | tf_op jit(solution)/shard_map/pallas_call | solution.py:189
  47.2 5.4 %all-to-all-done.1.along_ref = bf16[16,4,16,256]{3,2,1,0:T(8,128)(2,1)S(1)} async-done(((bf16[16,4,16,256]{3,2,1,0:T(8,128)(2,1)}), bf16[16,4,16,256]{3,2,1,0:T(8,128)(2,1)S(1)}, u32[]{:S(2)}, u32[]{:S(2)}) %all-to-all-start.1) | async-done | bytes 524320 | tf_op jit(solution)/shard_map/all_to_all | solution.py:335
  52.7 4.1 %all-to-all-start.3 = ((bf16[16,4,16,256]{3,2,1,0:T(8,128)(2,1)}), bf16[16,4,16,256]{3,2,1,0:T(8,128)(2,1)S(1)}, u32[]{:S(2)}, u32[]{:S(2)}) async-start(bf16[16,4,16,256]{3,2,1,0:T(8,128)(2,1)} %shard_map.106), calls=%async_computation.3 | async-start | bytes 1048576 | tf_op jit(solution)/shard_map/all_to_all | solution.py:343
  56.8 0.2 shard_map.104.modes_ref
  57.0 1.6 %collective-permute-start = (bf16[1,64,256]{2,1,0:T(8,128)(2,1)S(1)}, bf16[1,64,256]{2,1,0:T(8,128)(2,1)S(1)}, u32[]{:S(2)}, u32[]{:S(2)}) collective-permute-start(bf16[1,64,256]{2,1,0:T(8,128)(2,1)S(1)} %slice_select_fusion), channel_id=1, source_target_pairs={{0,1},{1,0},{2,3},{3,2},{4,5},{5,4},{6,7},{7,6},{8,9},{9,8},{10,11... | collective-permute-start | bytes 98312 | tf_op jit(solution)/shard_map/ppermute | solution.py:302
  58.6 0.0 copy-done.7
  58.6 0.1 copy.15
  58.7 0.0 copy-done.5
  58.7 0.1 copy.16
  58.8 0.0 copy-done.6
  58.8 0.1 copy.18
  59.0 2.0 %collective-permute-done = bf16[1,64,256]{2,1,0:T(8,128)(2,1)S(1)} collective-permute-done((bf16[1,64,256]{2,1,0:T(8,128)(2,1)S(1)}, bf16[1,64,256]{2,1,0:T(8,128)(2,1)S(1)}, u32[]{:S(2)}, u32[]{:S(2)}) %collective-permute-start) | collective-permute-done | bytes 32800 | tf_op jit(solution)/shard_map/ppermute | solution.py:302
  61.0 5.0 %shard_map.105 = bf16[16,4,16,256]{3,2,1,0:T(8,128)(2,1)} custom-call(bf16[1,64,256]{2,1,0:T(8,128)(2,1)S(1)} %get-tuple-element.16.below_ref, bf16[4,64,256]{2,1,0:T(8,128)(2,1)S(1)} %shard_map.104.modes_ref, bf16[1,64,256]{2,1,0:T(8,128)(2,1)S(1)} %get-tuple-element.15.above_ref, bf16[64,192,256]{2,1,0:T(8,128)(2,1)} %shard_map.101.weight_ref, ...), custom_call_target="tpu_custom_call" | custom-call | flops 25165824 | bytes 6291456 | tf_op jit(solution)/shard_map/pallas_call | solution.py:189
  66.0 5.2 %all-to-all-done.3.back_ref = bf16[16,4,16,256]{3,2,1,0:T(8,128)(2,1)S(1)} async-done(((bf16[16,4,16,256]{3,2,1,0:T(8,128)(2,1)}), bf16[16,4,16,256]{3,2,1,0:T(8,128)(2,1)S(1)}, u32[]{:S(2)}, u32[]{:S(2)}) %all-to-all-start.3) | async-done | bytes 524320 | tf_op jit(solution)/shard_map/all_to_all | solution.py:343
  71.2 4.1 %all-to-all-start.2 = ((bf16[16,4,16,256]{3,2,1,0:T(8,128)(2,1)}), bf16[16,4,16,256]{3,2,1,0:T(8,128)(2,1)S(1)}, u32[]{:S(2)}, u32[]{:S(2)}) async-start(bf16[16,4,16,256]{3,2,1,0:T(8,128)(2,1)} %shard_map.105), calls=%async_computation.2 | async-start | bytes 1048576 | tf_op jit(solution)/shard_map/all_to_all | solution.py:343
  75.4 0.0 copy-done.8
  75.4 0.1 broadcast_in_dim.2.bias_ref
  75.5 0.0 copy-done.4
  75.5 33.6 %shard_map.107.rest_0_ = bf16[2,4,16,64,1024]{4,3,2,1,0:T(8,128)(2,1)} custom-call(bf16[2,4,16,64,1024]{4,3,2,1,0:T(8,128)(2,1)} %field_ref.7, bf16[16,4,16,256]{3,2,1,0:T(8,128)(2,1)S(1)} %all-to-all-done.3.back_ref, bf16[64,1024]{1,0:T(8,128)(2,1)S(1)} %copy-done.1, bf16[64,64]{1,0:T(8,128)(2,1)S(1)} %bitcast.4, f32[64,256]{1,0:T(8,128)S(1)} %broadcast_in_dim.2.bias_ref, ...), custom_call_target="tpu_custom_call" | custom-call | flops 7516192768 | bytes 16777216 | tf_op jit(solution)/shard_map/pallas_call | solution.py:281
  109.1 0.0 all-to-all-done.2.back_ref
  109.1 33.6 %shard_map.108 = bf16[2,4,16,64,1024]{4,3,2,1,0:T(8,128)(2,1)} custom-call(bf16[2,4,16,64,1024]{4,3,2,1,0:T(8,128)(2,1)} %field_ref.7, bf16[16,4,16,256]{3,2,1,0:T(8,128)(2,1)S(1)} %all-to-all-done.2.back_ref, bf16[64,1024]{1,0:T(8,128)(2,1)S(1)} %copy-done.1, bf16[64,64]{1,0:T(8,128)(2,1)S(1)} %bitcast.5, ...), custom_call_target="tpu_custom_call", output_to_operand_aliasing={{}: (7, {})} | custom-call | flops 7516192768 | bytes 16777216 | tf_op jit(solution)/shard_map/pallas_call | solution.py:281
  (6 shorter events, 0.1 us)
Async XLA Ops:
  0.0 0.9 copy-start
  0.9 24.2 %copy-start.1 = (bf16[64,1024]{1,0:T(8,128)(2,1)S(1)}, bf16[64,1024]{1,0:T(8,128)(2,1)}, u32[]{:S(2)}) copy-start(bf16[64,1024]{1,0:T(8,128)(2,1)} %constant.16.clone.lon_ref) | copy-start | bytes 393220
  7.7 24.2 %all-to-all-start = ((bf16[16,4,16,256]{3,2,1,0:T(8,128)(2,1)}), bf16[16,4,16,256]{3,2,1,0:T(8,128)(2,1)S(1)}, u32[]{:S(2)}, u32[]{:S(2)}) async-start(bf16[16,4,16,256]{3,2,1,0:T(8,128)(2,1)} %shard_map.100), calls=%async_computation | async-start | bytes 1048576 | tf_op jit(solution)/shard_map/all_to_all | solution.py:335
  15.1 16.9 %copy-start.3 = (bf16[128,256]{1,0:T(8,128)(2,1)S(1)}, bf16[128,256]{1,0:T(8,128)(2,1)}, u32[]{:S(2)}) copy-start(bf16[128,256]{1,0:T(8,128)(2,1)} %constant.17.clone.table_ref) | copy-start | bytes 196612
  15.1 27.1 %copy-start.2 = (bf16[256,128]{1,0:T(8,128)(2,1)S(1)}, bf16[256,128]{1,0:T(8,128)(2,1)}, u32[]{:S(2)}) copy-start(bf16[256,128]{1,0:T(8,128)(2,1)} %constant.18.clone.table_ref) | copy-start | bytes 196612
  25.1 33.5 %copy-start.7 = (bf16[64,64]{1,0:T(8,128)(2,1)S(1)}, bf16[64,64]{1,0:T(8,128)(2,1)}, u32[]{:S(2)}) copy-start(bf16[64,64]{1,0:T(8,128)(2,1)} %param.12) | copy-start | bytes 24580
  25.1 33.6 %copy-start.5 = (bf16[64,256]{1,0:T(8,128)(2,1)S(1)}, bf16[64,256]{1,0:T(8,128)(2,1)}, u32[]{:S(2)}) copy-start(bf16[64,256]{1,0:T(8,128)(2,1)} %param.14) | copy-start | bytes 98308
  25.1 33.7 %copy-start.6 = (bf16[64,256]{1,0:T(8,128)(2,1)S(1)}, bf16[64,256]{1,0:T(8,128)(2,1)}, u32[]{:S(2)}) copy-start(bf16[64,256]{1,0:T(8,128)(2,1)} %param.15) | copy-start | bytes 98308
  25.1 50.3 %copy-start.8 = (f32[64]{0:T(128)S(1)}, f32[64]{0:T(128)}, u32[]{:S(2)}) copy-start(f32[64]{0:T(128)} %param.13) | copy-start | bytes 772
  25.1 50.4 %copy-start.4 = (bf16[256,64]{0,1:T(8,128)(2,1)S(1)}, bf16[256,64]{0,1:T(8,128)(2,1)}, u32[]{:S(2)}) copy-start(bf16[256,64]{0,1:T(8,128)(2,1)} %param.16) | copy-start | bytes 98308
  32.2 20.5 %all-to-all-start.1 = ((bf16[16,4,16,256]{3,2,1,0:T(8,128)(2,1)}), bf16[16,4,16,256]{3,2,1,0:T(8,128)(2,1)S(1)}, u32[]{:S(2)}, u32[]{:S(2)}) async-start(bf16[16,4,16,256]{3,2,1,0:T(8,128)(2,1)} %shard_map.103), calls=%async_computation.1 | async-start | bytes 1048576 | tf_op jit(solution)/shard_map/all_to_all | solution.py:335
  38.2 4.0 %collective-permute-start.1 = (bf16[1,64,256]{2,1,0:T(8,128)(2,1)S(1)}, bf16[1,64,256]{2,1,0:T(8,128)(2,1)S(1)}, u32[]{:S(2)}, u32[]{:S(2)}) collective-permute-start(bf16[1,64,256]{2,1,0:T(8,128)(2,1)S(1)} %slice_select_fusion.1), channel_id=1, source_target_pairs={{0,1},{1,0},{2,3},{3,2},{4,5},{5,4},{6,7},{7,6},{8,9},{9,8},{10,11... | collective-permute-start | bytes 98312 | tf_op jit(solution)/shard_map/ppermute | solution.py:302
  52.7 18.6 %all-to-all-start.3 = ((bf16[16,4,16,256]{3,2,1,0:T(8,128)(2,1)}), bf16[16,4,16,256]{3,2,1,0:T(8,128)(2,1)S(1)}, u32[]{:S(2)}, u32[]{:S(2)}) async-start(bf16[16,4,16,256]{3,2,1,0:T(8,128)(2,1)} %shard_map.106), calls=%async_computation.3 | async-start | bytes 1048576 | tf_op jit(solution)/shard_map/all_to_all | solution.py:343
  57.0 4.0 %collective-permute-start = (bf16[1,64,256]{2,1,0:T(8,128)(2,1)S(1)}, bf16[1,64,256]{2,1,0:T(8,128)(2,1)S(1)}, u32[]{:S(2)}, u32[]{:S(2)}) collective-permute-start(bf16[1,64,256]{2,1,0:T(8,128)(2,1)S(1)} %slice_select_fusion), channel_id=1, source_target_pairs={{0,1},{1,0},{2,3},{3,2},{4,5},{5,4},{6,7},{7,6},{8,9},{9,8},{10,11... | collective-permute-start | bytes 98312 | tf_op jit(solution)/shard_map/ppermute | solution.py:302
  71.2 37.8 %all-to-all-start.2 = ((bf16[16,4,16,256]{3,2,1,0:T(8,128)(2,1)}), bf16[16,4,16,256]{3,2,1,0:T(8,128)(2,1)S(1)}, u32[]{:S(2)}, u32[]{:S(2)}) async-start(bf16[16,4,16,256]{3,2,1,0:T(8,128)(2,1)} %shard_map.105), calls=%async_computation.2 | async-start | bytes 1048576 | tf_op jit(solution)/shard_map/all_to_all | solution.py:343

commit v3 on v2

--- a/solution.py
+++ b/solution.py
@@ -27,7 +27,7 @@
     return high, low
 
 
-def call(kernel, grid, in_specs, out_specs, out_shape, scratch, flops, moved, **kw):
+def call(kernel, grid, in_specs, out_specs, out_shape, scratch, flops, moved, room=48, **kw):
     return pl.pallas_call(
         kernel,
         grid=grid,
@@ -36,7 +36,7 @@
         out_shape=out_shape,
         scratch_shapes=scratch,
         compiler_params=pltpu.CompilerParams(
-            dimension_semantics=("arbitrary",) * len(grid), vmem_limit_bytes=48 * 2**20
+            dimension_semantics=("arbitrary",) * len(grid), vmem_limit_bytes=room * 2**20
         ),
         cost_estimate=pl.CostEstimate(flops=flops, bytes_accessed=moved, transcendentals=0),
         **kw,
@@ -93,6 +93,7 @@
         [lanes(rows * ranks, wide)],
         2 * levels * rows * chans * cells * modes,
         levels * rows * chans * cells * 2,
+        room=60,
     )(field, lon_rows)
 
 
@@ -132,8 +133,9 @@
             )
 
 
-def arrange(weight, part=8):
+def arrange(weight, part=32):
     shifts, lat_modes, band, chans, outs = weight.shape
+    part = math.gcd(part, lat_modes)
     return call(
         arrange_kernel,
         (lat_modes // part,),
@@ -205,90 +207,145 @@
 
 
 def finish_kernel(
-    ahead, field_ref, back_ref, lon_ref, local_ref, bias_ref, into_ref, down_ref, *rest
+    batch_at, ahead, back_ref, lon_ref, local_ref, bias_ref, into_ref, down_ref, field_ref, *rest
 ):
-    out_ref, held, coarse, act, hidden = rest[-5:]
-    ranks, _, rows, wide = back_ref.shape
+    out_ref, held, coarse, act, hidden, taken, given, take_sem, give_sem = rest[-9:]
+    ranks, levels, rows, wide = back_ref.shape
     chans, cells = field_ref.shape[3:]
     band = wide // chans
     hid = down_ref.shape[1]
+    total = levels * rows
+    steps = total // ahead
+    slots, kept = taken.shape[0], given.shape[0]
     tile = min(256, cells)
     spans = [slice(x, x + tile) for x in range(0, cells, tile)]
 
-    put(held, slice(None), back_ref[:, 0].astype(F32).reshape(ranks * rows, wide))
-    for n in range(rows):
-        piece = every(held, n, ranks, rows)
+    def take(t):
+        slot = lax.rem(t, slots)
+        source = field_ref.at[batch_at, t // rows, lax.rem(t, rows)]
+        return pltpu.make_async_copy(source, taken.at[slot], take_sem.at[slot])
+
+    def give(t):
+        slot = lax.rem(t, kept)
+        target = out_ref.at[batch_at, t // rows, lax.rem(t, rows)]
+        return pltpu.make_async_copy(given.at[slot], target, give_sem.at[slot])
+
+    for t in range(min(slots - ahead, total)):
+        take(jnp.int32(t)).start()
+
+    for l in range(levels):
+        put(
+            held,
+            slice(l * ranks * rows, (l + 1) * ranks * rows),
+            back_ref[:, l].astype(F32).reshape(ranks * rows, wide),
+        )
+
+    def prepare(u, t):
+        t = jnp.minimum(t, total - 1)
+        piece = every(held, (t // rows) * (ranks * rows) + lax.rem(t, rows), ranks, rows)
         stacked = jnp.concatenate(
             [piece[:, j * chans : (j + 1) * chans] for j in range(band)], axis=0
         )
-        coarse[n] = jnp.concatenate([stacked.T.astype(BF), local_ref[...]], axis=1)
-
-    def first(n, span):
-        cells_in = jnp.concatenate([lon_ref[:, span], field_ref[0, 0, n, :, span]], axis=0)
-        return jnp.dot(coarse[n], cells_in, preferred_element_type=F32)
+        coarse[u] = jnp.concatenate([stacked.T.astype(BF), local_ref[...]], axis=1)
+
+    def first(u, slot, span):
+        both = jnp.concatenate([lon_ref[:, span], taken[slot, :, span]], axis=0)
+        return jnp.dot(coarse[u], both, preferred_element_type=F32)
 
     def store_act(u, span, value):
         value = value + bias_ref[...]
         half = 0.5 * value
         act[u, :, span] = (half + half * lax.erf(value * math.sqrt(0.5))).astype(BF)
 
-    def last(u, n, span):
+    def last(u, slot, into, span):
         down = jnp.dot(down_ref[...], hidden[u, :, span], preferred_element_type=F32)
-        out_ref[0, 0, n, :, span] = (field_ref[0, 0, n, :, span].astype(F32) + down).astype(BF)
+        given[into, :, span] = (taken[slot, :, span].astype(F32) + down).astype(BF)
 
     for u in range(ahead):
+        prepare(u, jnp.int32(u))
+    for u in range(ahead):
+        take(jnp.int32(u)).wait()
         for span in spans:
-            store_act(u, span, first(u, span))
-
-    def one(t, carry):
+            store_act(u, span, first(u, u, span))
+    for u in range(ahead):
+        prepare(u, jnp.int32(ahead + u))
+
+    def one(step, carry):
+        t = step * ahead
+
+        @pl.when(step + 1 < steps)
+        def _():
+            for u in range(ahead):
+                take(t + ahead + u).wait()
+
+        @pl.when(t - ahead - kept >= 0)
+        def _():
+            for u in range(ahead):
+                give(t - ahead - kept + u).wait()
+
         for u in range(ahead):
-            n = t * ahead + u
+            before = t - ahead + u + slots * kept
             for span in spans:
                 both = jnp.dot(into_ref[...], act[u, :, span], preferred_element_type=F32)
-                last(u, jnp.maximum(n - ahead, 0), span)
-                value = first(jnp.minimum(n + ahead, rows - 1), span)
+                last(u, lax.rem(before, slots), lax.rem(before, kept), span)
+                value = first(u, lax.rem(t + ahead + u, slots), span)
                 half = both[:hid]
                 hidden[u, :, span] = ((half + half * jnp.tanh(half)) * both[hid:]).astype(BF)
                 store_act(u, span, value)
+            prepare(u, t + 2 * ahead + u)
+
+        @pl.when(step > 0)
+        def _():
+            for u in range(ahead):
+                give(t - ahead + u).start()
+
+        @pl.when(t - ahead + slots < total)
+        def _():
+            for u in range(ahead):
+                take(t - ahead + slots + u).start()
+
         return carry
 
-    lax.fori_loop(0, rows // ahead, one, 0)
+    lax.fori_loop(0, steps, one, 0)
     for u in range(ahead):
+        t = total - ahead + u
+        if t >= kept:
+            give(jnp.int32(t - kept)).wait()
         for span in spans:
-            last(u, rows - ahead + u, span)
+            last(u, t % slots, t % kept, span)
+        give(jnp.int32(t)).start()
+    for t in range(max(total - kept, 0), total):
+        give(jnp.int32(t)).wait()
 
 
 def finish(field, back, lon_rows, local, bias, into, down, batch_at, earlier, ahead=2):
     batch, levels, rows, chans, cells = field.shape
     ranks, _, _, wide = back.shape
     modes = lon_rows.shape[0]
-    spot = pl.BlockSpec((1, 1, rows, chans, cells), lambda l: (batch_at, l, 0, 0, 0))
-    operands = [field, back, lon_rows, local, bias, into, down]
-    in_specs = [
-        spot,
-        pl.BlockSpec((ranks, 1, rows, wide), lambda l: (0, l, 0, 0)),
-        whole(lon_rows.shape),
-        whole(local.shape),
-        whole(bias.shape),
-        whole(into.shape),
-        whole(down.shape),
-    ]
+    slots, kept = 8 * ahead, 2 * ahead
+    operands = [back, lon_rows, local, bias, into, down, field]
+    anywhere = pl.BlockSpec(memory_space=pl.ANY)
+    in_specs = [whole(x.shape) for x in operands[:-1]] + [anywhere]
     kw = {}
     if earlier is not None:
         operands.append(earlier)
-        in_specs.append(pl.BlockSpec(memory_space=pl.ANY))
+        in_specs.append(anywhere)
         kw["input_output_aliases"] = {7: 0}
     return call(
-        functools.partial(finish_kernel, ahead),
-        (levels,),
+        functools.partial(finish_kernel, batch_at, ahead),
+        (1,),
         in_specs,
-        spot,
+        anywhere,
         jax.ShapeDtypeStruct(field.shape, BF),
         [
-            lanes(ranks * rows, wide),
-            pltpu.VMEM((rows, chans, modes + chans), BF),
+            lanes(levels * ranks * rows, wide),
+            pltpu.VMEM((ahead, chans, modes + chans), BF),
             pltpu.VMEM((ahead, chans, cells), BF),
             pltpu.VMEM((ahead, down.shape[1], cells), BF),
+            pltpu.VMEM((slots, chans, cells), BF),
+            pltpu.VMEM((kept, chans, cells), BF),
+            pltpu.SemaphoreType.DMA((slots,)),
+            pltpu.SemaphoreType.DMA((kept,)),
         ],
         2 * levels * rows * cells * chans * (modes + chans + 3 * down.shape[1]),
         levels * rows * chans * cells * 4,

time: 143 us -> 134 us (0.937)
  Pallas kernels: 101 us -> 92.8 us
    pallas_call x2, Pallas kernels: 67.1 us -> 61.3 us  [finish(): call(functools.partial(finish_kernel, batch_at, ahead), (1,), in_specs, a...]
    pallas_call x1, Pallas kernels: 10 us -> 7.19 us  [arrange(): call(arrange_kernel, (lat_modes // part,), [pl.BlockSpec((shifts, part, b...]
  transfers between devices with their start and end apart: 6 -> 6, of which waited for: 4 -> 5; matrix products, arithmetic and copies ran while one was open for 0% -> 0% of each run, Pallas kernels for 43% -> 41%
where the time goes in v3:
time: 134 us; the launch traced here: 133 us
  Pallas kernels  92.8 us (69%)
  starting transfers between devices  24.7 us (18%)
  waiting for transfers between devices  15.2 us (11%)
    pallas_call x2, Pallas kernels, finish(): call(functools.partial(finish_kernel, batch_at, ahead), (1,), in_specs, a...  61.3 us
    pallas_call x2, Pallas kernels, forward(): call(functools.partial(forward_kernel, ranks), (levels,), [pl.BlockSpec((...  13.9 us
    all_to_all x2, starting transfers between devices, body(): along = lax.all_to_all(sent[b], 'rows', 0, 0, tiled=True)  13.3 us
    pallas_call x2, Pallas kernels, mix(): call(mix_kernel, (1,), [whole(below.shape), whole(modes.shape), whole(abo...  10 us
    all_to_all x2, starting transfers between devices, body(): backs.append(lax.all_to_all(back, 'rows', 0, 0, tiled=True))  8.2 us
    pallas_call x1, Pallas kernels, arrange(): call(arrange_kernel, (lat_modes // part,), [pl.BlockSpec((shifts, part, b...  7.19 us
    all_to_all x2, waiting for transfers between devices, body(): along = lax.all_to_all(sent[b], 'rows', 0, 0, tiled=True)  5.52 us
    all_to_all x2, waiting for transfers between devices, body(): backs.append(lax.all_to_all(back, 'rows', 0, 0, tiled=True))  5.22 us
  transfers between devices with their start and end apart: 6, of which 5 were waited for; matrix products, arithmetic and copies ran while one was open for 0% of the time, Pallas kernels for 41%

profile of v3, /device:TPU:0, one launch (start us, length us, event | category | flops | bytes accessed | tf_op | source)
XLA Modules:
  0.0 133.3 jit_solution(11865596497446886018)
XLA Ops:
  0.0 6.7 %shard_map.100 = bf16[16,4,16,256]{3,2,1,0:T(8,128)(2,1)} custom-call(bf16[2,4,16,64,1024]{4,3,2,1,0:T(8,128)(2,1)} %field_ref.7, bf16[64,1024]{1,0:T(8,128)(2,1)} %constant.16.clone.lon_ref), custom_call_target="tpu_custom_call" | custom-call | flops 536870912 | bytes 8388608 | tf_op jit(solution)/shard_map/pallas_call | solution.py:84
  6.7 7.4 %all-to-all-start = ((bf16[16,4,16,256]{3,2,1,0:T(8,128)(2,1)}), bf16[16,4,16,256]{3,2,1,0:T(8,128)(2,1)S(1)}, u32[]{:S(2)}, u32[]{:S(2)}) async-start(bf16[16,4,16,256]{3,2,1,0:T(8,128)(2,1)} %shard_map.100), calls=%async_computation | async-start | bytes 1048576 | tf_op jit(solution)/shard_map/all_to_all | solution.py:392
  14.1 0.0 copy-start.2
  14.1 0.0 copy-start.1
  14.1 7.2 %shard_map.101.weight_ref = bf16[64,192,256]{2,1,0:T(8,128)(2,1)} custom-call(bf16[3,64,4,64,64]{4,3,2,1,0:T(8,128)(2,1)} %weight_ref.1), custom_call_target="tpu_custom_call" | custom-call | flops 3145728 | bytes 18874368 | tf_op jit(solution)/shard_map/pallas_call | solution.py:139
  21.3 0.0 copy-start.6
  21.3 0.0 copy-start.4
  21.3 0.0 copy-start.5
  21.3 0.0 copy-start.7
  21.3 0.0 copy-start
  21.4 0.0 copy-start.3
  21.4 7.1 %shard_map.103 = bf16[16,4,16,256]{3,2,1,0:T(8,128)(2,1)} custom-call(bf16[2,4,16,64,1024]{4,3,2,1,0:T(8,128)(2,1)} %field_ref.7, bf16[64,1024]{1,0:T(8,128)(2,1)} %constant.16.clone.lon_ref), custom_call_target="tpu_custom_call" | custom-call | flops 536870912 | bytes 8388608 | tf_op jit(solution)/shard_map/pallas_call | solution.py:84
  28.5 0.1 all-to-all-done.along_ref
  28.6 0.0 copy-done.2
  28.6 0.2 shard_map.102.modes_ref
  28.8 5.9 %all-to-all-start.1 = ((bf16[16,4,16,256]{3,2,1,0:T(8,128)(2,1)}), bf16[16,4,16,256]{3,2,1,0:T(8,128)(2,1)S(1)}, u32[]{:S(2)}, u32[]{:S(2)}) async-start(bf16[16,4,16,256]{3,2,1,0:T(8,128)(2,1)} %shard_map.103), calls=%async_computation.1 | async-start | bytes 1048576 | tf_op jit(solution)/shard_map/all_to_all | solution.py:392
  34.8 1.6 %collective-permute-start.1 = (bf16[1,64,256]{2,1,0:T(8,128)(2,1)S(1)}, bf16[1,64,256]{2,1,0:T(8,128)(2,1)S(1)}, u32[]{:S(2)}, u32[]{:S(2)}) collective-permute-start(bf16[1,64,256]{2,1,0:T(8,128)(2,1)S(1)} %slice_select_fusion.1), channel_id=1, source_target_pairs={{0,1},{1,0},{2,3},{3,2},{4,5},{5,4},{6,7},{7,6},{8,9},{9,8},{10,11... | collective-permute-start | bytes 98312 | tf_op jit(solution)/shard_map/ppermute | solution.py:359
  36.4 2.4 %collective-permute-done.1 = bf16[1,64,256]{2,1,0:T(8,128)(2,1)S(1)} collective-permute-done((bf16[1,64,256]{2,1,0:T(8,128)(2,1)S(1)}, bf16[1,64,256]{2,1,0:T(8,128)(2,1)S(1)}, u32[]{:S(2)}, u32[]{:S(2)}) %collective-permute-start.1) | collective-permute-done | bytes 32800 | tf_op jit(solution)/shard_map/ppermute | solution.py:359
  38.8 0.0 copy-done.1
  38.8 5.0 %shard_map.106 = bf16[16,4,16,256]{3,2,1,0:T(8,128)(2,1)} custom-call(bf16[1,64,256]{2,1,0:T(8,128)(2,1)S(1)} %get-tuple-element.14.below_ref, bf16[4,64,256]{2,1,0:T(8,128)(2,1)S(1)} %shard_map.102.modes_ref, bf16[1,64,256]{2,1,0:T(8,128)(2,1)S(1)} %get-tuple-element.13.above_ref, bf16[64,192,256]{2,1,0:T(8,128)(2,1)} %shard_map.101.weight_ref, ...), custom_call_target="tpu_custom_call" | custom-call | flops 25165824 | bytes 6291456 | tf_op jit(solution)/shard_map/pallas_call | solution.py:191
  43.8 5.4 %all-to-all-done.1.along_ref = bf16[16,4,16,256]{3,2,1,0:T(8,128)(2,1)S(1)} async-done(((bf16[16,4,16,256]{3,2,1,0:T(8,128)(2,1)}), bf16[16,4,16,256]{3,2,1,0:T(8,128)(2,1)S(1)}, u32[]{:S(2)}, u32[]{:S(2)}) %all-to-all-start.1) | async-done | bytes 524320 | tf_op jit(solution)/shard_map/all_to_all | solution.py:392
  49.2 4.1 %all-to-all-start.3 = ((bf16[16,4,16,256]{3,2,1,0:T(8,128)(2,1)}), bf16[16,4,16,256]{3,2,1,0:T(8,128)(2,1)S(1)}, u32[]{:S(2)}, u32[]{:S(2)}) async-start(bf16[16,4,16,256]{3,2,1,0:T(8,128)(2,1)} %shard_map.106), calls=%async_computation.3 | async-start | bytes 1048576 | tf_op jit(solution)/shard_map/all_to_all | solution.py:400
  53.3 0.2 shard_map.104.modes_ref
  53.6 1.6 %collective-permute-start = (bf16[1,64,256]{2,1,0:T(8,128)(2,1)S(1)}, bf16[1,64,256]{2,1,0:T(8,128)(2,1)S(1)}, u32[]{:S(2)}, u32[]{:S(2)}) collective-permute-start(bf16[1,64,256]{2,1,0:T(8,128)(2,1)S(1)} %slice_select_fusion), channel_id=1, source_target_pairs={{0,1},{1,0},{2,3},{3,2},{4,5},{5,4},{6,7},{7,6},{8,9},{9,8},{10,11... | collective-permute-start | bytes 98312 | tf_op jit(solution)/shard_map/ppermute | solution.py:359
  55.2 0.0 copy-done.6
  55.2 0.1 copy.15
  55.3 0.0 copy-done.4
  55.3 0.1 copy.16
  55.4 0.0 copy-done.5
  55.4 0.1 copy.18
  55.5 2.0 %collective-permute-done = bf16[1,64,256]{2,1,0:T(8,128)(2,1)S(1)} collective-permute-done((bf16[1,64,256]{2,1,0:T(8,128)(2,1)S(1)}, bf16[1,64,256]{2,1,0:T(8,128)(2,1)S(1)}, u32[]{:S(2)}, u32[]{:S(2)}) %collective-permute-start) | collective-permute-done | bytes 32800 | tf_op jit(solution)/shard_map/ppermute | solution.py:359
  57.6 5.0 %shard_map.105 = bf16[16,4,16,256]{3,2,1,0:T(8,128)(2,1)} custom-call(bf16[1,64,256]{2,1,0:T(8,128)(2,1)S(1)} %get-tuple-element.16.below_ref, bf16[4,64,256]{2,1,0:T(8,128)(2,1)S(1)} %shard_map.104.modes_ref, bf16[1,64,256]{2,1,0:T(8,128)(2,1)S(1)} %get-tuple-element.15.above_ref, bf16[64,192,256]{2,1,0:T(8,128)(2,1)} %shard_map.101.weight_ref, ...), custom_call_target="tpu_custom_call" | custom-call | flops 25165824 | bytes 6291456 | tf_op jit(solution)/shard_map/pallas_call | solution.py:191
  62.6 5.2 %all-to-all-done.3.back_ref = bf16[16,4,16,256]{3,2,1,0:T(8,128)(2,1)S(1)} async-done(((bf16[16,4,16,256]{3,2,1,0:T(8,128)(2,1)}), bf16[16,4,16,256]{3,2,1,0:T(8,128)(2,1)S(1)}, u32[]{:S(2)}, u32[]{:S(2)}) %all-to-all-start.3) | async-done | bytes 524320 | tf_op jit(solution)/shard_map/all_to_all | solution.py:400
  67.8 4.1 %all-to-all-start.2 = ((bf16[16,4,16,256]{3,2,1,0:T(8,128)(2,1)}), bf16[16,4,16,256]{3,2,1,0:T(8,128)(2,1)S(1)}, u32[]{:S(2)}, u32[]{:S(2)}) async-start(bf16[16,4,16,256]{3,2,1,0:T(8,128)(2,1)} %shard_map.105), calls=%async_computation.2 | async-start | bytes 1048576 | tf_op jit(solution)/shard_map/all_to_all | solution.py:400
  72.0 0.0 copy-done.7
  72.0 0.1 broadcast_in_dim.2.bias_ref
  72.0 0.0 copy-done
  72.0 0.0 copy-done.3
  72.1 30.6 %shard_map.107.rest_0_ = bf16[2,4,16,64,1024]{4,3,2,1,0:T(8,128)(2,1)} custom-call(bf16[16,4,16,256]{3,2,1,0:T(8,128)(2,1)S(1)} %all-to-all-done.3.back_ref, bf16[64,1024]{1,0:T(8,128)(2,1)S(1)} %copy-done, bf16[64,64]{1,0:T(8,128)(2,1)S(1)} %bitcast.4, f32[64,256]{1,0:T(8,128)S(1)} %broadcast_in_dim.2.bias_ref, ...), custom_call_target="tpu_custom_call" | custom-call | flops 7516192768 | bytes 16777216 | tf_op jit(solution)/shard_map/pallas_call | solution.py:334
  102.7 0.0 all-to-all-done.2.back_ref
  102.7 30.6 %shard_map.108 = bf16[2,4,16,64,1024]{4,3,2,1,0:T(8,128)(2,1)} custom-call(bf16[16,4,16,256]{3,2,1,0:T(8,128)(2,1)S(1)} %all-to-all-done.2.back_ref, bf16[64,1024]{1,0:T(8,128)(2,1)S(1)} %copy-done, bf16[64,64]{1,0:T(8,128)(2,1)S(1)} %bitcast.5, f32[64,256]{1,0:T(8,128)S(1)} %broadcast_in_dim.2.bias_ref, ...), custom_call_target="tpu_custom_call", output_to_operand_aliasing={{}: (7, {})} | custom-call | flops 7516192768 | bytes 16777216 | tf_op jit(solution)/shard_map/pallas_call | solution.py:334
  (6 shorter events, 0.1 us)
Async XLA Ops:
  6.7 21.8 %all-to-all-start = ((bf16[16,4,16,256]{3,2,1,0:T(8,128)(2,1)}), bf16[16,4,16,256]{3,2,1,0:T(8,128)(2,1)S(1)}, u32[]{:S(2)}, u32[]{:S(2)}) async-start(bf16[16,4,16,256]{3,2,1,0:T(8,128)(2,1)} %shard_map.100), calls=%async_computation | async-start | bytes 1048576 | tf_op jit(solution)/shard_map/all_to_all | solution.py:392
  14.1 14.5 %copy-start.2 = (bf16[128,256]{1,0:T(8,128)(2,1)S(1)}, bf16[128,256]{1,0:T(8,128)(2,1)}, u32[]{:S(2)}) copy-start(bf16[128,256]{1,0:T(8,128)(2,1)} %constant.17.clone.table_ref) | copy-start | bytes 196612
  14.1 24.6 %copy-start.1 = (bf16[256,128]{1,0:T(8,128)(2,1)S(1)}, bf16[256,128]{1,0:T(8,128)(2,1)}, u32[]{:S(2)}) copy-start(bf16[256,128]{1,0:T(8,128)(2,1)} %constant.18.clone.table_ref) | copy-start | bytes 196612
  21.3 33.8 %copy-start.6 = (bf16[64,64]{1,0:T(8,128)(2,1)S(1)}, bf16[64,64]{1,0:T(8,128)(2,1)}, u32[]{:S(2)}) copy-start(bf16[64,64]{1,0:T(8,128)(2,1)} %param.12) | copy-start | bytes 24580
  21.3 33.9 %copy-start.4 = (bf16[64,256]{1,0:T(8,128)(2,1)S(1)}, bf16[64,256]{1,0:T(8,128)(2,1)}, u32[]{:S(2)}) copy-start(bf16[64,256]{1,0:T(8,128)(2,1)} %param.14) | copy-start | bytes 98308
  21.3 34.1 %copy-start.5 = (bf16[64,256]{1,0:T(8,128)(2,1)S(1)}, bf16[64,256]{1,0:T(8,128)(2,1)}, u32[]{:S(2)}) copy-start(bf16[64,256]{1,0:T(8,128)(2,1)} %param.15) | copy-start | bytes 98308
  21.3 50.6 %copy-start.7 = (f32[64]{0:T(128)S(1)}, f32[64]{0:T(128)}, u32[]{:S(2)}) copy-start(f32[64]{0:T(128)} %param.13) | copy-start | bytes 772
  21.3 50.7 %copy-start = (bf16[64,1024]{1,0:T(8,128)(2,1)S(1)}, bf16[64,1024]{1,0:T(8,128)(2,1)}, u32[]{:S(2)}) copy-start(bf16[64,1024]{1,0:T(8,128)(2,1)} %constant.16.clone.lon_ref) | copy-start | bytes 393220
  21.4 50.7 %copy-start.3 = (bf16[256,64]{0,1:T(8,128)(2,1)S(1)}, bf16[256,64]{0,1:T(8,128)(2,1)}, u32[]{:S(2)}) copy-start(bf16[256,64]{0,1:T(8,128)(2,1)} %param.16) | copy-start | bytes 98308
  28.8 20.4 %all-to-all-start.1 = ((bf16[16,4,16,256]{3,2,1,0:T(8,128)(2,1)}), bf16[16,4,16,256]{3,2,1,0:T(8,128)(2,1)S(1)}, u32[]{:S(2)}, u32[]{:S(2)}) async-start(bf16[16,4,16,256]{3,2,1,0:T(8,128)(2,1)} %shard_map.103), calls=%async_computation.1 | async-start | bytes 1048576 | tf_op jit(solution)/shard_map/all_to_all | solution.py:392
  34.8 4.0 %collective-permute-start.1 = (bf16[1,64,256]{2,1,0:T(8,128)(2,1)S(1)}, bf16[1,64,256]{2,1,0:T(8,128)(2,1)S(1)}, u32[]{:S(2)}, u32[]{:S(2)}) collective-permute-start(bf16[1,64,256]{2,1,0:T(8,128)(2,1)S(1)} %slice_select_fusion.1), channel_id=1, source_target_pairs={{0,1},{1,0},{2,3},{3,2},{4,5},{5,4},{6,7},{7,6},{8,9},{9,8},{10,11... | collective-permute-start | bytes 98312 | tf_op jit(solution)/shard_map/ppermute | solution.py:359
  49.2 18.6 %all-to-all-start.3 = ((bf16[16,4,16,256]{3,2,1,0:T(8,128)(2,1)}), bf16[16,4,16,256]{3,2,1,0:T(8,128)(2,1)S(1)}, u32[]{:S(2)}, u32[]{:S(2)}) async-start(bf16[16,4,16,256]{3,2,1,0:T(8,128)(2,1)} %shard_map.106), calls=%async_computation.3 | async-start | bytes 1048576 | tf_op jit(solution)/shard_map/all_to_all | solution.py:400
  53.6 4.0 %collective-permute-start = (bf16[1,64,256]{2,1,0:T(8,128)(2,1)S(1)}, bf16[1,64,256]{2,1,0:T(8,128)(2,1)S(1)}, u32[]{:S(2)}, u32[]{:S(2)}) collective-permute-start(bf16[1,64,256]{2,1,0:T(8,128)(2,1)S(1)} %slice_select_fusion), channel_id=1, source_target_pairs={{0,1},{1,0},{2,3},{3,2},{4,5},{5,4},{6,7},{7,6},{8,9},{9,8},{10,11... | collective-permute-start | bytes 98312 | tf_op jit(solution)/shard_map/ppermute | solution.py:359
  67.8 34.9 %all-to-all-start.2 = ((bf16[16,4,16,256]{3,2,1,0:T(8,128)(2,1)}), bf16[16,4,16,256]{3,2,1,0:T(8,128)(2,1)S(1)}, u32[]{:S(2)}, u32[]{:S(2)}) async-start(bf16[16,4,16,256]{3,2,1,0:T(8,128)(2,1)} %shard_map.105), calls=%async_computation.2 | async-start | bytes 1048576 | tf_op jit(solution)/shard_map/all_to_all | solution.py:400

commit v4 on v3

--- a/solution.py
+++ b/solution.py
@@ -12,6 +12,7 @@
 
 BF = jnp.bfloat16
 F32 = jnp.float32
+F8 = jnp.float8_e4m3fn
 NT = (((1,), (1,)), ((), ()))
 
 
@@ -43,6 +44,21 @@
     )
 
 
+def power(bound):
+    scale, back = jnp.full_like(bound, 2.0**-40), jnp.full_like(bound, 2.0**40)
+    for step in (64, 32, 16, 8, 4, 2, 1):
+        more = scale * 2.0**step
+        fits = bound * more <= 256.0
+        scale = jnp.where(fits, more, scale)
+        back = jnp.where(fits, back * 2.0**-step, back)
+    return scale, back
+
+
+def pieces(value):
+    high = value.astype(F8)
+    return high, (value - high.astype(value.dtype)).astype(F8)
+
+
 def lanes(rows, wide):
     return pltpu.VMEM((wide // 128, rows, 128), F32)
 
@@ -62,7 +78,7 @@
     return pl.BlockSpec(shape, lambda *_: (0,) * len(shape))
 
 
-def forward_kernel(ranks, field_ref, lon_ref, out_ref, held):
+def forward_kernel(ranks, field_ref, lon_ref, out_ref, loud_ref, held):
     _, _, rows, chans, cells = field_ref.shape
     modes = lon_ref.shape[0]
     band = modes // ranks
@@ -75,6 +91,11 @@
         put(held, pl.ds(n * ranks, ranks), row)
     for r in range(ranks):
         out_ref[r, 0] = every(held, r, rows, ranks).astype(BF)
+    size = jnp.abs(field_ref[0, 0]).reshape(rows, chans // 16, 16, cells)
+    size = functools.reduce(jnp.maximum, [size[:, i] for i in range(chans // 16)])
+    size = functools.reduce(jnp.maximum, [size[..., x : x + 128] for x in range(0, cells, 128)])
+    size = jnp.max(size.astype(F32), axis=(1, 2), keepdims=True)
+    loud_ref[0] = jnp.broadcast_to(size, (rows, 1, 128)).reshape(rows, 128)
 
 
 def forward(field, lon_rows, batch_at, ranks):
@@ -88,8 +109,14 @@
             pl.BlockSpec((1, 1, rows, chans, cells), lambda l: (batch_at, l, 0, 0, 0)),
             whole((modes, cells)),
         ],
-        pl.BlockSpec((ranks, 1, rows, wide), lambda l: (0, l, 0, 0)),
-        jax.ShapeDtypeStruct((ranks, levels, rows, wide), BF),
+        [
+            pl.BlockSpec((ranks, 1, rows, wide), lambda l: (0, l, 0, 0)),
+            pl.BlockSpec((1, rows, 128), lambda l: (l, 0, 0)),
+        ],
+        [
+            jax.ShapeDtypeStruct((ranks, levels, rows, wide), BF),
+            jax.ShapeDtypeStruct((levels, rows, 128), F32),
+        ],
         [lanes(rows * ranks, wide)],
         2 * levels * rows * chans * cells * modes,
         levels * rows * chans * cells * 2,
@@ -207,9 +234,13 @@
 
 
 def finish_kernel(
-    batch_at, ahead, back_ref, lon_ref, local_ref, bias_ref, into_ref, down_ref, field_ref, *rest
+    batch_at, ahead, reach, back_ref, lon_ref, local_ref, bias_ref, into_ref, down_ref, loud_ref,
+    field_ref, *rest
 ):
-    out_ref, held, coarse, act, hidden, taken, given, take_sem, give_sem = rest[-9:]
+    (
+        out_ref, held, coarse, act, hidden, into, act_scale, gate_scale, up_scale,
+        taken, given, take_sem, give_sem,
+    ) = rest[-13:]
     ranks, levels, rows, wide = back_ref.shape
     chans, cells = field_ref.shape[3:]
     band = wide // chans
@@ -240,6 +271,33 @@
             back_ref[:, l].astype(F32).reshape(ranks * rows, wide),
         )
 
+    def largest(x):
+        return jnp.max(jnp.abs(x.astype(F32)), axis=(0, 1), keepdims=True)
+
+    inverse = []
+    for part in range(2):
+        weight = into_ref[part * hid : (part + 1) * hid].astype(F32)
+        scale, undo = power(largest(weight))
+        inverse.append(undo)
+        high, low = pieces(weight * scale)
+        high, low = high.astype(F32), low.astype(F32)
+        into[part * hid : (part + 1) * hid] = jnp.concatenate(
+            [high, high, low, low], axis=1
+        ).astype(F8)
+    mixing = jnp.max(
+        jnp.sum(jnp.abs(local_ref[...].astype(F32)), axis=1, keepdims=True), axis=0, keepdims=True
+    )
+    offset = largest(bias_ref[...])
+    for l in range(levels):
+        coarsest = functools.reduce(jnp.maximum, [jnp.abs(back_ref[r, l]) for r in range(ranks)])
+        coarsest = jnp.max(coarsest.astype(F32), axis=1, keepdims=True)
+        bound = 1.01 * (coarsest * reach + loud_ref[l] * mixing + offset)
+        scale, undo = power(jnp.concatenate([bound] * (tile // 128), axis=1))
+        at = slice(l * rows, (l + 1) * rows)
+        act_scale[at] = 0.5 * scale
+        gate_scale[at] = undo * inverse[0]
+        up_scale[at] = undo * inverse[1]
+
     def prepare(u, t):
         t = jnp.minimum(t, total - 1)
         piece = every(held, (t // rows) * (ranks * rows) + lax.rem(t, rows), ranks, rows)
@@ -252,21 +310,24 @@
         both = jnp.concatenate([lon_ref[:, span], taken[slot, :, span]], axis=0)
         return jnp.dot(coarse[u], both, preferred_element_type=F32)
 
-    def store_act(u, span, value):
+    def store_act(u, t, span, value):
         value = value + bias_ref[...]
-        half = 0.5 * value
-        act[u, :, span] = (half + half * lax.erf(value * math.sqrt(0.5))).astype(BF)
-
-    def last(u, slot, into, span):
+        half = value * act_scale[pl.ds(t, 1), :]
+        high, low = pieces((half + half * lax.erf(value * math.sqrt(0.5))).astype(BF))
+        act[u, :chans, span] = high
+        act[u, chans:, span] = low
+
+    def last(u, t, slot, kept_at, span):
         down = jnp.dot(down_ref[...], hidden[u, :, span], preferred_element_type=F32)
-        given[into, :, span] = (taken[slot, :, span].astype(F32) + down).astype(BF)
+        down = down * up_scale[pl.ds(t, 1), :]
+        given[kept_at, :, span] = (taken[slot, :, span].astype(F32) + down).astype(BF)
 
     for u in range(ahead):
         prepare(u, jnp.int32(u))
     for u in range(ahead):
         take(jnp.int32(u)).wait()
         for span in spans:
-            store_act(u, span, first(u, u, span))
+            store_act(u, u, span, first(u, u, span))
     for u in range(ahead):
         prepare(u, jnp.int32(ahead + u))
 
@@ -285,13 +346,18 @@
 
         for u in range(ahead):
             before = t - ahead + u + slots * kept
+            earlier = jnp.maximum(t - ahead + u, 0)
+            later = jnp.minimum(t + ahead + u, total - 1)
+            gate_undo = gate_scale[pl.ds(t + u, 1), :].astype(BF)
             for span in spans:
-                both = jnp.dot(into_ref[...], act[u, :, span], preferred_element_type=F32)
-                last(u, lax.rem(before, slots), lax.rem(before, kept), span)
+                ours = act[u, :, span]
+                ours = jnp.concatenate([ours, ours], axis=0)
+                both = jnp.dot(into[...], ours, preferred_element_type=F32)
+                last(u, earlier, lax.rem(before, slots), lax.rem(before, kept), span)
                 value = first(u, lax.rem(t + ahead + u, slots), span)
-                half = both[:hid]
-                hidden[u, :, span] = ((half + half * jnp.tanh(half)) * both[hid:]).astype(BF)
-                store_act(u, span, value)
+                half = both[:hid].astype(BF) * gate_undo
+                hidden[u, :, span] = half * (1 + jnp.tanh(half)) * both[hid:].astype(BF)
+                store_act(u, later, span, value)
             prepare(u, t + 2 * ahead + u)
 
         @pl.when(step > 0)
@@ -312,27 +378,27 @@
         if t >= kept:
             give(jnp.int32(t - kept)).wait()
         for span in spans:
-            last(u, t % slots, t % kept, span)
+            last(u, t, t % slots, t % kept, span)
         give(jnp.int32(t)).start()
     for t in range(max(total - kept, 0), total):
         give(jnp.int32(t)).wait()
 
 
-def finish(field, back, lon_rows, local, bias, into, down, batch_at, earlier, ahead=2):
+def finish(field, back, lon_rows, local, bias, into, down, loud, reach, batch_at, earlier, ahead=2):
     batch, levels, rows, chans, cells = field.shape
     ranks, _, _, wide = back.shape
     modes = lon_rows.shape[0]
     slots, kept = 8 * ahead, 2 * ahead
-    operands = [back, lon_rows, local, bias, into, down, field]
+    operands = [back, lon_rows, local, bias, into, down, loud, field]
     anywhere = pl.BlockSpec(memory_space=pl.ANY)
     in_specs = [whole(x.shape) for x in operands[:-1]] + [anywhere]
     kw = {}
     if earlier is not None:
         operands.append(earlier)
         in_specs.append(anywhere)
-        kw["input_output_aliases"] = {7: 0}
+        kw["input_output_aliases"] = {8: 0}
     return call(
-        functools.partial(finish_kernel, batch_at, ahead),
+        functools.partial(finish_kernel, batch_at, ahead, reach),
         (1,),
         in_specs,
         anywhere,
@@ -340,8 +406,10 @@
         [
             lanes(levels * ranks * rows, wide),
             pltpu.VMEM((ahead, chans, modes + chans), BF),
-            pltpu.VMEM((ahead, chans, cells), BF),
+            pltpu.VMEM((ahead, 2 * chans, cells), F8),
             pltpu.VMEM((ahead, down.shape[1], cells), BF),
+            pltpu.VMEM((2 * down.shape[1], 4 * chans), F8),
+            *[pltpu.VMEM((levels * rows, min(256, cells)), F32)] * 3,
             pltpu.VMEM((slots, chans, cells), BF),
             pltpu.VMEM((kept, chans, cells), BF),
             pltpu.SemaphoreType.DMA((slots,)),
@@ -375,6 +443,7 @@
     lon_modes = band * ranks
     lon_rows = cas_table(cells, lon_modes).astype(ml_dtypes.bfloat16).T
     lon_rows = lon_rows.reshape(ranks, band, cells).swapaxes(0, 1).reshape(lon_modes, cells)
+    reach = float(np.abs(lon_rows.astype(np.float32)).sum(axis=0).max())
     lon_rows = jnp.asarray(np.ascontiguousarray(lon_rows))
     high, low = split(cas_table(rows * ranks, lat_modes))
     gather_table = jnp.asarray(np.concatenate([high.T, low.T], axis=0))
@@ -386,7 +455,7 @@
     bias = jnp.broadcast_to(local_bias[:, None], (chans, min(256, cells)))
 
     weight = arrange(spectral_weight)
-    sent = [forward(field, lon_rows, b, ranks) for b in range(batch)]
+    sent, loud = map(list, zip(*[forward(field, lon_rows, b, ranks) for b in range(batch)]))
     backs = []
     for b in range(batch):
         along = lax.all_to_all(sent[b], "rows", 0, 0, tiled=True)
@@ -400,7 +469,9 @@
         backs.append(lax.all_to_all(back, "rows", 0, 0, tiled=True))
     result = None
     for b in range(batch):
-        result = finish(field, backs[b], lon_rows, local, bias, into, down, b, result)
+        result = finish(
+            field, backs[b], lon_rows, local, bias, into, down, loud[b], reach, b, result
+        )
     return result
 
 

time: 134 us -> 127 us (0.948)
  Pallas kernels: 92.8 us -> 85.4 us
    pallas_call x2, Pallas kernels: 61.3 us -> 53.5 us  [finish(): call(functools.partial(finish_kernel, batch_at, ahead, reach), (1,), in_s...]
  transfers between devices with their start and end apart: 6 -> 6, of which waited for: 5 -> 4; matrix products, arithmetic and copies ran while one was open for 0% -> 0% of each run, Pallas kernels for 41% -> 41%
where the time goes in v4:
time: 127 us; the launch traced here: 126 us
  Pallas kernels  85.4 us (67%)
  starting transfers between devices  24.7 us (19%)
  waiting for transfers between devices  15.1 us (12%)
    pallas_call x2, Pallas kernels, finish(): call(functools.partial(finish_kernel, batch_at, ahead, reach), (1,), in_s...  53.5 us
    pallas_call x2, Pallas kernels, forward(): call(functools.partial(forward_kernel, ranks), (levels,), [pl.BlockSpec((...  14.3 us
    all_to_all x2, starting transfers between devices, body(): along = lax.all_to_all(sent[b], 'rows', 0, 0, tiled=True)  13.4 us
    pallas_call x2, Pallas kernels, mix(): call(mix_kernel, (1,), [whole(below.shape), whole(modes.shape), whole(abo...  10 us
    all_to_all x2, starting transfers between devices, body(): backs.append(lax.all_to_all(back, 'rows', 0, 0, tiled=True))  8.2 us
    pallas_call x1, Pallas kernels, arrange(): call(arrange_kernel, (lat_modes // part,), [pl.BlockSpec((shifts, part, b...  7.19 us
    all_to_all x2, waiting for transfers between devices, body(): along = lax.all_to_all(sent[b], 'rows', 0, 0, tiled=True)  5.44 us
    all_to_all x2, waiting for transfers between devices, body(): backs.append(lax.all_to_all(back, 'rows', 0, 0, tiled=True))  5.21 us
  transfers between devices with their start and end apart: 6, of which 4 were waited for; matrix products, arithmetic and copies ran while one was open for 0% of the time, Pallas kernels for 41%

profile of v4, /device:TPU:0, one launch (start us, length us, event | category | flops | bytes accessed | tf_op | source)
XLA Modules:
  0.0 126.0 jit_solution(17917111500730808869)
XLA Ops:
  0.0 7.0 %shard_map.100 = (bf16[16,4,16,256]{3,2,1,0:T(8,128)(2,1)}, f32[4,16,128]{2,1,0:T(8,128)}) custom-call(bf16[2,4,16,64,1024]{4,3,2,1,0:T(8,128)(2,1)} %field_ref.7, bf16[64,1024]{1,0:T(8,128)(2,1)} %constant.16.clone.lon_ref), custom_call_target="tpu_custom_call" | custom-call | flops 536870912 | bytes 8388608 | tf_op jit(solution)/shard_map/pallas_call | solution.py:105
  7.0 7.4 %all-to-all-start = ((bf16[16,4,16,256]{3,2,1,0:T(8,128)(2,1)}), bf16[16,4,16,256]{3,2,1,0:T(8,128)(2,1)S(1)}, u32[]{:S(2)}, u32[]{:S(2)}) async-start(bf16[16,4,16,256]{3,2,1,0:T(8,128)(2,1)} %get-tuple-element.13), calls=%async_computation | async-start | bytes 1048576 | tf_op jit(solution)/shard_map/all_to_all | solution.py:461
  14.4 0.0 copy-start.2
  14.4 0.0 copy-start.1
  14.4 7.2 %shard_map.101.weight_ref = bf16[64,192,256]{2,1,0:T(8,128)(2,1)} custom-call(bf16[3,64,4,64,64]{4,3,2,1,0:T(8,128)(2,1)} %weight_ref.1), custom_call_target="tpu_custom_call" | custom-call | flops 3145728 | bytes 18874368 | tf_op jit(solution)/shard_map/pallas_call | solution.py:166
  21.6 0.0 copy-start.8
  21.6 0.0 copy-start.6
  21.6 0.0 copy-start.7
  21.6 0.0 copy-start.9
  21.6 0.0 copy-start
  21.6 0.0 copy-start.3
  21.6 0.0 copy-start.5
  21.6 7.3 %shard_map.103 = (bf16[16,4,16,256]{3,2,1,0:T(8,128)(2,1)}, f32[4,16,128]{2,1,0:T(8,128)}) custom-call(bf16[2,4,16,64,1024]{4,3,2,1,0:T(8,128)(2,1)} %field_ref.7, bf16[64,1024]{1,0:T(8,128)(2,1)} %constant.16.clone.lon_ref), custom_call_target="tpu_custom_call" | custom-call | flops 536870912 | bytes 8388608 | tf_op jit(solution)/shard_map/pallas_call | solution.py:105
  28.9 0.0 all-to-all-done.along_ref
  28.9 0.0 copy-done.2
  29.0 0.2 shard_map.102.modes_ref
  29.2 6.0 %all-to-all-start.1 = ((bf16[16,4,16,256]{3,2,1,0:T(8,128)(2,1)}), bf16[16,4,16,256]{3,2,1,0:T(8,128)(2,1)S(1)}, u32[]{:S(2)}, u32[]{:S(2)}) async-start(bf16[16,4,16,256]{3,2,1,0:T(8,128)(2,1)} %get-tuple-element.16), calls=%async_computation.1 | async-start | bytes 1048576 | tf_op jit(solution)/shard_map/all_to_all | solution.py:461
  35.2 1.6 %collective-permute-start.1 = (bf16[1,64,256]{2,1,0:T(8,128)(2,1)S(1)}, bf16[1,64,256]{2,1,0:T(8,128)(2,1)S(1)}, u32[]{:S(2)}, u32[]{:S(2)}) collective-permute-start(bf16[1,64,256]{2,1,0:T(8,128)(2,1)S(1)} %slice_select_fusion.1), channel_id=1, source_target_pairs={{0,1},{1,0},{2,3},{3,2},{4,5},{5,4},{6,7},{7,6},{8,9},{9,8},{10,11... | collective-permute-start | bytes 98312 | tf_op jit(solution)/shard_map/ppermute | solution.py:427
  36.8 2.4 %collective-permute-done.1 = bf16[1,64,256]{2,1,0:T(8,128)(2,1)S(1)} collective-permute-done((bf16[1,64,256]{2,1,0:T(8,128)(2,1)S(1)}, bf16[1,64,256]{2,1,0:T(8,128)(2,1)S(1)}, u32[]{:S(2)}, u32[]{:S(2)}) %collective-permute-start.1) | collective-permute-done | bytes 32800 | tf_op jit(solution)/shard_map/ppermute | solution.py:427
  39.2 0.0 copy-done.1
  39.2 5.0 %shard_map.106 = bf16[16,4,16,256]{3,2,1,0:T(8,128)(2,1)} custom-call(bf16[1,64,256]{2,1,0:T(8,128)(2,1)S(1)} %get-tuple-element.22.below_ref, bf16[4,64,256]{2,1,0:T(8,128)(2,1)S(1)} %shard_map.102.modes_ref, bf16[1,64,256]{2,1,0:T(8,128)(2,1)S(1)} %get-tuple-element.21.above_ref, bf16[64,192,256]{2,1,0:T(8,128)(2,1)} %shard_map.101.weight_ref, ...), custom_call_target="tpu_custom_call" | custom-call | flops 25165824 | bytes 6291456 | tf_op jit(solution)/shard_map/pallas_call | solution.py:218
  44.2 5.4 %all-to-all-done.1.along_ref = bf16[16,4,16,256]{3,2,1,0:T(8,128)(2,1)S(1)} async-done(((bf16[16,4,16,256]{3,2,1,0:T(8,128)(2,1)}), bf16[16,4,16,256]{3,2,1,0:T(8,128)(2,1)S(1)}, u32[]{:S(2)}, u32[]{:S(2)}) %all-to-all-start.1) | async-done | bytes 524320 | tf_op jit(solution)/shard_map/all_to_all | solution.py:461
  49.7 4.1 %all-to-all-start.3 = ((bf16[16,4,16,256]{3,2,1,0:T(8,128)(2,1)}), bf16[16,4,16,256]{3,2,1,0:T(8,128)(2,1)S(1)}, u32[]{:S(2)}, u32[]{:S(2)}) async-start(bf16[16,4,16,256]{3,2,1,0:T(8,128)(2,1)} %shard_map.106), calls=%async_computation.3 | async-start | bytes 1048576 | tf_op jit(solution)/shard_map/all_to_all | solution.py:469
  53.8 0.2 shard_map.104.modes_ref
  54.0 1.6 %collective-permute-start = (bf16[1,64,256]{2,1,0:T(8,128)(2,1)S(1)}, bf16[1,64,256]{2,1,0:T(8,128)(2,1)S(1)}, u32[]{:S(2)}, u32[]{:S(2)}) collective-permute-start(bf16[1,64,256]{2,1,0:T(8,128)(2,1)S(1)} %slice_select_fusion), channel_id=1, source_target_pairs={{0,1},{1,0},{2,3},{3,2},{4,5},{5,4},{6,7},{7,6},{8,9},{9,8},{10,11... | collective-permute-start | bytes 98312 | tf_op jit(solution)/shard_map/ppermute | solution.py:427
  55.6 0.0 copy-done.8
  55.6 0.1 copy.15
  55.7 0.0 copy-done.6
  55.7 0.1 copy.16
  55.9 0.0 copy-done.7
  55.9 0.1 copy.18
  56.0 2.0 %collective-permute-done = bf16[1,64,256]{2,1,0:T(8,128)(2,1)S(1)} collective-permute-done((bf16[1,64,256]{2,1,0:T(8,128)(2,1)S(1)}, bf16[1,64,256]{2,1,0:T(8,128)(2,1)S(1)}, u32[]{:S(2)}, u32[]{:S(2)}) %collective-permute-start) | collective-permute-done | bytes 32800 | tf_op jit(solution)/shard_map/ppermute | solution.py:427
  58.0 5.0 %shard_map.105 = bf16[16,4,16,256]{3,2,1,0:T(8,128)(2,1)} custom-call(bf16[1,64,256]{2,1,0:T(8,128)(2,1)S(1)} %get-tuple-element.24.below_ref, bf16[4,64,256]{2,1,0:T(8,128)(2,1)S(1)} %shard_map.104.modes_ref, bf16[1,64,256]{2,1,0:T(8,128)(2,1)S(1)} %get-tuple-element.23.above_ref, bf16[64,192,256]{2,1,0:T(8,128)(2,1)} %shard_map.101.weight_ref, ...), custom_call_target="tpu_custom_call" | custom-call | flops 25165824 | bytes 6291456 | tf_op jit(solution)/shard_map/pallas_call | solution.py:218
  63.0 5.2 %all-to-all-done.3.back_ref = bf16[16,4,16,256]{3,2,1,0:T(8,128)(2,1)S(1)} async-done(((bf16[16,4,16,256]{3,2,1,0:T(8,128)(2,1)}), bf16[16,4,16,256]{3,2,1,0:T(8,128)(2,1)S(1)}, u32[]{:S(2)}, u32[]{:S(2)}) %all-to-all-start.3) | async-done | bytes 524320 | tf_op jit(solution)/shard_map/all_to_all | solution.py:469
  68.3 4.1 %all-to-all-start.2 = ((bf16[16,4,16,256]{3,2,1,0:T(8,128)(2,1)}), bf16[16,4,16,256]{3,2,1,0:T(8,128)(2,1)S(1)}, u32[]{:S(2)}, u32[]{:S(2)}) async-start(bf16[16,4,16,256]{3,2,1,0:T(8,128)(2,1)} %shard_map.105), calls=%async_computation.2 | async-start | bytes 1048576 | tf_op jit(solution)/shard_map/all_to_all | solution.py:469
  72.4 0.0 copy-done.9
  72.4 0.1 broadcast_in_dim.2.bias_ref
  72.5 0.0 copy-done
  72.5 0.0 copy-done.3
  72.5 0.0 copy-done.5
  72.5 0.0 copy-start.4
  72.5 26.7 %shard_map.107.rest_0_ = bf16[2,4,16,64,1024]{4,3,2,1,0:T(8,128)(2,1)} custom-call(bf16[16,4,16,256]{3,2,1,0:T(8,128)(2,1)S(1)} %all-to-all-done.3.back_ref, bf16[64,1024]{1,0:T(8,128)(2,1)S(1)} %copy-done, bf16[64,64]{1,0:T(8,128)(2,1)S(1)} %bitcast.4, f32[64,256]{1,0:T(8,128)S(1)} %broadcast_in_dim.2.bias_ref, ...), custom_call_target="tpu_custom_call" | custom-call | flops 7516192768 | bytes 16777216 | tf_op jit(solution)/shard_map/pallas_call | solution.py:400
  99.3 0.0 all-to-all-done.2.back_ref
  99.3 0.0 copy-done.4
  99.3 26.8 %shard_map.108 = bf16[2,4,16,64,1024]{4,3,2,1,0:T(8,128)(2,1)} custom-call(bf16[16,4,16,256]{3,2,1,0:T(8,128)(2,1)S(1)} %all-to-all-done.2.back_ref, bf16[64,1024]{1,0:T(8,128)(2,1)S(1)} %copy-done, bf16[64,64]{1,0:T(8,128)(2,1)S(1)} %bitcast.5, f32[64,256]{1,0:T(8,128)S(1)} %broadcast_in_dim.2.bias_ref, ...), custom_call_target="tpu_custom_call", output_to_operand_aliasing={{}: (8, {})} | custom-call | flops 7516192768 | bytes 16777216 | tf_op jit(solution)/shard_map/pallas_call | solution.py:400
  (6 shorter events, 0.1 us)
Async XLA Ops:
  7.0 21.9 %all-to-all-start = ((bf16[16,4,16,256]{3,2,1,0:T(8,128)(2,1)}), bf16[16,4,16,256]{3,2,1,0:T(8,128)(2,1)S(1)}, u32[]{:S(2)}, u32[]{:S(2)}) async-start(bf16[16,4,16,256]{3,2,1,0:T(8,128)(2,1)} %get-tuple-element.13), calls=%async_computation | async-start | bytes 1048576 | tf_op jit(solution)/shard_map/all_to_all | solution.py:461
  14.4 14.6 %copy-start.2 = (bf16[128,256]{1,0:T(8,128)(2,1)S(1)}, bf16[128,256]{1,0:T(8,128)(2,1)}, u32[]{:S(2)}) copy-start(bf16[128,256]{1,0:T(8,128)(2,1)} %constant.17.clone.table_ref) | copy-start | bytes 196612
  14.4 24.8 %copy-start.1 = (bf16[256,128]{1,0:T(8,128)(2,1)S(1)}, bf16[256,128]{1,0:T(8,128)(2,1)}, u32[]{:S(2)}) copy-start(bf16[256,128]{1,0:T(8,128)(2,1)} %constant.18.clone.table_ref) | copy-start | bytes 196612
  21.6 34.0 %copy-start.8 = (bf16[64,64]{1,0:T(8,128)(2,1)S(1)}, bf16[64,64]{1,0:T(8,128)(2,1)}, u32[]{:S(2)}) copy-start(bf16[64,64]{1,0:T(8,128)(2,1)} %param.12) | copy-start | bytes 24580
  21.6 34.1 %copy-start.6 = (bf16[64,256]{1,0:T(8,128)(2,1)S(1)}, bf16[64,256]{1,0:T(8,128)(2,1)}, u32[]{:S(2)}) copy-start(bf16[64,256]{1,0:T(8,128)(2,1)} %param.14) | copy-start | bytes 98308
  21.6 34.3 %copy-start.7 = (bf16[64,256]{1,0:T(8,128)(2,1)S(1)}, bf16[64,256]{1,0:T(8,128)(2,1)}, u32[]{:S(2)}) copy-start(bf16[64,256]{1,0:T(8,128)(2,1)} %param.15) | copy-start | bytes 98308
  21.6 50.8 %copy-start.9 = (f32[64]{0:T(128)S(1)}, f32[64]{0:T(128)}, u32[]{:S(2)}) copy-start(f32[64]{0:T(128)} %param.13) | copy-start | bytes 772
  21.6 50.9 %copy-start = (bf16[64,1024]{1,0:T(8,128)(2,1)S(1)}, bf16[64,1024]{1,0:T(8,128)(2,1)}, u32[]{:S(2)}) copy-start(bf16[64,1024]{1,0:T(8,128)(2,1)} %constant.16.clone.lon_ref) | copy-start | bytes 393220
  21.6 50.9 %copy-start.3 = (bf16[256,64]{0,1:T(8,128)(2,1)S(1)}, bf16[256,64]{0,1:T(8,128)(2,1)}, u32[]{:S(2)}) copy-start(bf16[256,64]{0,1:T(8,128)(2,1)} %param.16) | copy-start | bytes 98308
  21.6 50.9 %copy-start.5 = (f32[4,16,128]{2,1,0:T(8,128)S(1)}, f32[4,16,128]{2,1,0:T(8,128)}, u32[]{:S(2)}) copy-start(f32[4,16,128]{2,1,0:T(8,128)} %get-tuple-element.20.loud_ref) | copy-start | bytes 98308
  29.2 20.5 %all-to-all-start.1 = ((bf16[16,4,16,256]{3,2,1,0:T(8,128)(2,1)}), bf16[16,4,16,256]{3,2,1,0:T(8,128)(2,1)S(1)}, u32[]{:S(2)}, u32[]{:S(2)}) async-start(bf16[16,4,16,256]{3,2,1,0:T(8,128)(2,1)} %get-tuple-element.16), calls=%async_computation.1 | async-start | bytes 1048576 | tf_op jit(solution)/shard_map/all_to_all | solution.py:461
  35.2 4.0 %collective-permute-start.1 = (bf16[1,64,256]{2,1,0:T(8,128)(2,1)S(1)}, bf16[1,64,256]{2,1,0:T(8,128)(2,1)S(1)}, u32[]{:S(2)}, u32[]{:S(2)}) collective-permute-start(bf16[1,64,256]{2,1,0:T(8,128)(2,1)S(1)} %slice_select_fusion.1), channel_id=1, source_target_pairs={{0,1},{1,0},{2,3},{3,2},{4,5},{5,4},{6,7},{7,6},{8,9},{9,8},{10,11... | collective-permute-start | bytes 98312 | tf_op jit(solution)/shard_map/ppermute | solution.py:427
  49.7 18.6 %all-to-all-start.3 = ((bf16[16,4,16,256]{3,2,1,0:T(8,128)(2,1)}), bf16[16,4,16,256]{3,2,1,0:T(8,128)(2,1)S(1)}, u32[]{:S(2)}, u32[]{:S(2)}) async-start(bf16[16,4,16,256]{3,2,1,0:T(8,128)(2,1)} %shard_map.106), calls=%async_computation.3 | async-start | bytes 1048576 | tf_op jit(solution)/shard_map/all_to_all | solution.py:469
  54.0 4.0 %collective-permute-start = (bf16[1,64,256]{2,1,0:T(8,128)(2,1)S(1)}, bf16[1,64,256]{2,1,0:T(8,128)(2,1)S(1)}, u32[]{:S(2)}, u32[]{:S(2)}) collective-permute-start(bf16[1,64,256]{2,1,0:T(8,128)(2,1)S(1)} %slice_select_fusion), channel_id=1, source_target_pairs={{0,1},{1,0},{2,3},{3,2},{4,5},{5,4},{6,7},{7,6},{8,9},{9,8},{10,11... | collective-permute-start | bytes 98312 | tf_op jit(solution)/shard_map/ppermute | solution.py:427
  68.3 31.0 %all-to-all-start.2 = ((bf16[16,4,16,256]{3,2,1,0:T(8,128)(2,1)}), bf16[16,4,16,256]{3,2,1,0:T(8,128)(2,1)S(1)}, u32[]{:S(2)}, u32[]{:S(2)}) async-start(bf16[16,4,16,256]{3,2,1,0:T(8,128)(2,1)} %shard_map.105), calls=%async_computation.2 | async-start | bytes 1048576 | tf_op jit(solution)/shard_map/all_to_all | solution.py:469
  72.5 26.7 %copy-start.4 = (f32[4,16,128]{2,1,0:T(8,128)S(1)}, f32[4,16,128]{2,1,0:T(8,128)}, u32[]{:S(2)}) copy-start(f32[4,16,128]{2,1,0:T(8,128)} %get-tuple-element.18.loud_ref) | copy-start | bytes 98308

commit v5 on v4

--- a/solution.py
+++ b/solution.py
@@ -59,8 +59,8 @@
     return high, (value - high.astype(value.dtype)).astype(F8)
 
 
-def lanes(rows, wide):
-    return pltpu.VMEM((wide // 128, rows, 128), F32)
+def lanes(size, stride, wide):
+    return pltpu.VMEM((wide // 128, (size + 1) * stride, 128), F32)
 
 
 def every(ref, start, size, stride):
@@ -117,7 +117,7 @@
             jax.ShapeDtypeStruct((ranks, levels, rows, wide), BF),
             jax.ShapeDtypeStruct((levels, rows, 128), F32),
         ],
-        [lanes(rows * ranks, wide)],
+        [lanes(rows, ranks, wide)],
         2 * levels * rows * chans * cells * modes,
         levels * rows * chans * cells * 2,
         room=60,
@@ -180,7 +180,7 @@
     ranks, levels, rows, _ = out_ref.shape
     chans = deep // 3
     band = wide // chans
-    step = mixed.shape[1] // lat_modes
+    step = mixed.shape[1] // (lat_modes + 1)
 
     near = [below_ref[0].astype(F32)]
     near += [modes_ref[l].astype(F32) for l in range(levels)]
@@ -227,7 +227,7 @@
         ],
         whole((ranks, levels, rows, wide)),
         jax.ShapeDtypeStruct((ranks, levels, rows, wide), BF),
-        [lanes(lat_modes * step, (deep + 127) // 128 * 128), lanes(lat_modes * step, wide)],
+        [lanes(lat_modes, step, (deep + 127) // 128 * 128), lanes(lat_modes, step, wide)],
         weight.size * 2 * levels,
         weight.size * 2,
     )(below, modes, above, weight, table)
@@ -404,7 +404,7 @@
         anywhere,
         jax.ShapeDtypeStruct(field.shape, BF),
         [
-            lanes(levels * ranks * rows, wide),
+            lanes(levels * ranks, rows, wide),
             pltpu.VMEM((ahead, chans, modes + chans), BF),
             pltpu.VMEM((ahead, 2 * chans, cells), F8),
             pltpu.VMEM((ahead, down.shape[1], cells), BF),

time: 127 us -> 127 us (level)
  no operation moved by 1% of the time
where the time goes in v5:
time: 127 us; the launch traced here: 126 us
  Pallas kernels  85.4 us (67%)
  starting transfers between devices  24.7 us (19%)
  waiting for transfers between devices  15.1 us (12%)
    pallas_call x2, Pallas kernels, finish(): call(functools.partial(finish_kernel, batch_at, ahead, reach), (1,), in_s...  53.4 us
    pallas_call x2, Pallas kernels, forward(): call(functools.partial(forward_kernel, ranks), (levels,), [pl.BlockSpec((...  14.3 us
    all_to_all x2, starting transfers between devices, body(): along = lax.all_to_all(sent[b], 'rows', 0, 0, tiled=True)  13.4 us
    pallas_call x2, Pallas kernels, mix(): call(mix_kernel, (1,), [whole(below.shape), whole(modes.shape), whole(abo...  10 us
    all_to_all x2, starting transfers between devices, body(): backs.append(lax.all_to_all(back, 'rows', 0, 0, tiled=True))  8.2 us
    pallas_call x1, Pallas kernels, arrange(): call(arrange_kernel, (lat_modes // part,), [pl.BlockSpec((shifts, part, b...  7.19 us
    all_to_all x2, waiting for transfers between devices, body(): along = lax.all_to_all(sent[b], 'rows', 0, 0, tiled=True)  5.44 us
    all_to_all x2, waiting for transfers between devices, body(): backs.append(lax.all_to_all(back, 'rows', 0, 0, tiled=True))  5.21 us
  transfers between devices with their start and end apart: 6, of which 4 were waited for; matrix products, arithmetic and copies ran while one was open for 0% of the time, Pallas kernels for 41%

profile of v5, /device:TPU:0, one launch (start us, length us, event | category | flops | bytes accessed | tf_op | source)
XLA Modules:
  0.0 126.0 jit_solution(2026043905804465925)
XLA Ops:
  0.0 7.0 %shard_map.100 = (bf16[16,4,16,256]{3,2,1,0:T(8,128)(2,1)}, f32[4,16,128]{2,1,0:T(8,128)}) custom-call(bf16[2,4,16,64,1024]{4,3,2,1,0:T(8,128)(2,1)} %field_ref.7, bf16[64,1024]{1,0:T(8,128)(2,1)} %constant.16.clone.lon_ref), custom_call_target="tpu_custom_call" | custom-call | flops 536870912 | bytes 8388608 | tf_op jit(solution)/shard_map/pallas_call | solution.py:105
  7.0 7.4 %all-to-all-start = ((bf16[16,4,16,256]{3,2,1,0:T(8,128)(2,1)}), bf16[16,4,16,256]{3,2,1,0:T(8,128)(2,1)S(1)}, u32[]{:S(2)}, u32[]{:S(2)}) async-start(bf16[16,4,16,256]{3,2,1,0:T(8,128)(2,1)} %get-tuple-element.13), calls=%async_computation | async-start | bytes 1048576 | tf_op jit(solution)/shard_map/all_to_all | solution.py:461
  14.4 0.0 copy-start.2
  14.4 0.0 copy-start.1
  14.4 7.2 %shard_map.101.weight_ref = bf16[64,192,256]{2,1,0:T(8,128)(2,1)} custom-call(bf16[3,64,4,64,64]{4,3,2,1,0:T(8,128)(2,1)} %weight_ref.1), custom_call_target="tpu_custom_call" | custom-call | flops 3145728 | bytes 18874368 | tf_op jit(solution)/shard_map/pallas_call | solution.py:166
  21.6 0.0 copy-start.8
  21.6 0.0 copy-start.6
  21.6 0.0 copy-start.7
  21.6 0.0 copy-start.9
  21.6 0.0 copy-start
  21.6 0.0 copy-start.3
  21.6 0.0 copy-start.5
  21.6 7.3 %shard_map.103 = (bf16[16,4,16,256]{3,2,1,0:T(8,128)(2,1)}, f32[4,16,128]{2,1,0:T(8,128)}) custom-call(bf16[2,4,16,64,1024]{4,3,2,1,0:T(8,128)(2,1)} %field_ref.7, bf16[64,1024]{1,0:T(8,128)(2,1)} %constant.16.clone.lon_ref), custom_call_target="tpu_custom_call" | custom-call | flops 536870912 | bytes 8388608 | tf_op jit(solution)/shard_map/pallas_call | solution.py:105
  28.9 0.0 all-to-all-done.along_ref
  28.9 0.0 copy-done.2
  29.0 0.2 shard_map.102.modes_ref
  29.2 6.0 %all-to-all-start.1 = ((bf16[16,4,16,256]{3,2,1,0:T(8,128)(2,1)}), bf16[16,4,16,256]{3,2,1,0:T(8,128)(2,1)S(1)}, u32[]{:S(2)}, u32[]{:S(2)}) async-start(bf16[16,4,16,256]{3,2,1,0:T(8,128)(2,1)} %get-tuple-element.16), calls=%async_computation.1 | async-start | bytes 1048576 | tf_op jit(solution)/shard_map/all_to_all | solution.py:461
  35.2 1.6 %collective-permute-start.1 = (bf16[1,64,256]{2,1,0:T(8,128)(2,1)S(1)}, bf16[1,64,256]{2,1,0:T(8,128)(2,1)S(1)}, u32[]{:S(2)}, u32[]{:S(2)}) collective-permute-start(bf16[1,64,256]{2,1,0:T(8,128)(2,1)S(1)} %slice_select_fusion.1), channel_id=1, source_target_pairs={{0,1},{1,0},{2,3},{3,2},{4,5},{5,4},{6,7},{7,6},{8,9},{9,8},{10,11... | collective-permute-start | bytes 98312 | tf_op jit(solution)/shard_map/ppermute | solution.py:427
  36.8 2.4 %collective-permute-done.1 = bf16[1,64,256]{2,1,0:T(8,128)(2,1)S(1)} collective-permute-done((bf16[1,64,256]{2,1,0:T(8,128)(2,1)S(1)}, bf16[1,64,256]{2,1,0:T(8,128)(2,1)S(1)}, u32[]{:S(2)}, u32[]{:S(2)}) %collective-permute-start.1) | collective-permute-done | bytes 32800 | tf_op jit(solution)/shard_map/ppermute | solution.py:427
  39.2 0.0 copy-done.1
  39.2 5.0 %shard_map.106 = bf16[16,4,16,256]{3,2,1,0:T(8,128)(2,1)} custom-call(bf16[1,64,256]{2,1,0:T(8,128)(2,1)S(1)} %get-tuple-element.22.below_ref, bf16[4,64,256]{2,1,0:T(8,128)(2,1)S(1)} %shard_map.102.modes_ref, bf16[1,64,256]{2,1,0:T(8,128)(2,1)S(1)} %get-tuple-element.21.above_ref, bf16[64,192,256]{2,1,0:T(8,128)(2,1)} %shard_map.101.weight_ref, ...), custom_call_target="tpu_custom_call" | custom-call | flops 25165824 | bytes 6291456 | tf_op jit(solution)/shard_map/pallas_call | solution.py:218
  44.2 5.4 %all-to-all-done.1.along_ref = bf16[16,4,16,256]{3,2,1,0:T(8,128)(2,1)S(1)} async-done(((bf16[16,4,16,256]{3,2,1,0:T(8,128)(2,1)}), bf16[16,4,16,256]{3,2,1,0:T(8,128)(2,1)S(1)}, u32[]{:S(2)}, u32[]{:S(2)}) %all-to-all-start.1) | async-done | bytes 524320 | tf_op jit(solution)/shard_map/all_to_all | solution.py:461
  49.7 4.1 %all-to-all-start.3 = ((bf16[16,4,16,256]{3,2,1,0:T(8,128)(2,1)}), bf16[16,4,16,256]{3,2,1,0:T(8,128)(2,1)S(1)}, u32[]{:S(2)}, u32[]{:S(2)}) async-start(bf16[16,4,16,256]{3,2,1,0:T(8,128)(2,1)} %shard_map.106), calls=%async_computation.3 | async-start | bytes 1048576 | tf_op jit(solution)/shard_map/all_to_all | solution.py:469
  53.8 0.2 shard_map.104.modes_ref
  54.0 1.6 %collective-permute-start = (bf16[1,64,256]{2,1,0:T(8,128)(2,1)S(1)}, bf16[1,64,256]{2,1,0:T(8,128)(2,1)S(1)}, u32[]{:S(2)}, u32[]{:S(2)}) collective-permute-start(bf16[1,64,256]{2,1,0:T(8,128)(2,1)S(1)} %slice_select_fusion), channel_id=1, source_target_pairs={{0,1},{1,0},{2,3},{3,2},{4,5},{5,4},{6,7},{7,6},{8,9},{9,8},{10,11... | collective-permute-start | bytes 98312 | tf_op jit(solution)/shard_map/ppermute | solution.py:427
  55.6 0.0 copy-done.8
  55.6 0.1 copy.15
  55.7 0.0 copy-done.6
  55.7 0.1 copy.16
  55.9 0.0 copy-done.7
  55.9 0.1 copy.18
  56.0 2.0 %collective-permute-done = bf16[1,64,256]{2,1,0:T(8,128)(2,1)S(1)} collective-permute-done((bf16[1,64,256]{2,1,0:T(8,128)(2,1)S(1)}, bf16[1,64,256]{2,1,0:T(8,128)(2,1)S(1)}, u32[]{:S(2)}, u32[]{:S(2)}) %collective-permute-start) | collective-permute-done | bytes 32800 | tf_op jit(solution)/shard_map/ppermute | solution.py:427
  58.0 5.0 %shard_map.105 = bf16[16,4,16,256]{3,2,1,0:T(8,128)(2,1)} custom-call(bf16[1,64,256]{2,1,0:T(8,128)(2,1)S(1)} %get-tuple-element.24.below_ref, bf16[4,64,256]{2,1,0:T(8,128)(2,1)S(1)} %shard_map.104.modes_ref, bf16[1,64,256]{2,1,0:T(8,128)(2,1)S(1)} %get-tuple-element.23.above_ref, bf16[64,192,256]{2,1,0:T(8,128)(2,1)} %shard_map.101.weight_ref, ...), custom_call_target="tpu_custom_call" | custom-call | flops 25165824 | bytes 6291456 | tf_op jit(solution)/shard_map/pallas_call | solution.py:218
  63.0 5.2 %all-to-all-done.3.back_ref = bf16[16,4,16,256]{3,2,1,0:T(8,128)(2,1)S(1)} async-done(((bf16[16,4,16,256]{3,2,1,0:T(8,128)(2,1)}), bf16[16,4,16,256]{3,2,1,0:T(8,128)(2,1)S(1)}, u32[]{:S(2)}, u32[]{:S(2)}) %all-to-all-start.3) | async-done | bytes 524320 | tf_op jit(solution)/shard_map/all_to_all | solution.py:469
  68.3 4.1 %all-to-all-start.2 = ((bf16[16,4,16,256]{3,2,1,0:T(8,128)(2,1)}), bf16[16,4,16,256]{3,2,1,0:T(8,128)(2,1)S(1)}, u32[]{:S(2)}, u32[]{:S(2)}) async-start(bf16[16,4,16,256]{3,2,1,0:T(8,128)(2,1)} %shard_map.105), calls=%async_computation.2 | async-start | bytes 1048576 | tf_op jit(solution)/shard_map/all_to_all | solution.py:469
  72.4 0.0 copy-done.9
  72.4 0.1 broadcast_in_dim.2.bias_ref
  72.5 0.0 copy-done
  72.5 0.0 copy-done.3
  72.5 0.0 copy-done.5
  72.5 0.0 copy-start.4
  72.5 26.7 %shard_map.107.rest_0_ = bf16[2,4,16,64,1024]{4,3,2,1,0:T(8,128)(2,1)} custom-call(bf16[16,4,16,256]{3,2,1,0:T(8,128)(2,1)S(1)} %all-to-all-done.3.back_ref, bf16[64,1024]{1,0:T(8,128)(2,1)S(1)} %copy-done, bf16[64,64]{1,0:T(8,128)(2,1)S(1)} %bitcast.4, f32[64,256]{1,0:T(8,128)S(1)} %broadcast_in_dim.2.bias_ref, ...), custom_call_target="tpu_custom_call" | custom-call | flops 7516192768 | bytes 16777216 | tf_op jit(solution)/shard_map/pallas_call | solution.py:400
  99.2 0.0 all-to-all-done.2.back_ref
  99.2 0.0 copy-done.4
  99.2 26.7 %shard_map.108 = bf16[2,4,16,64,1024]{4,3,2,1,0:T(8,128)(2,1)} custom-call(bf16[16,4,16,256]{3,2,1,0:T(8,128)(2,1)S(1)} %all-to-all-done.2.back_ref, bf16[64,1024]{1,0:T(8,128)(2,1)S(1)} %copy-done, bf16[64,64]{1,0:T(8,128)(2,1)S(1)} %bitcast.5, f32[64,256]{1,0:T(8,128)S(1)} %broadcast_in_dim.2.bias_ref, ...), custom_call_target="tpu_custom_call", output_to_operand_aliasing={{}: (8, {})} | custom-call | flops 7516192768 | bytes 16777216 | tf_op jit(solution)/shard_map/pallas_call | solution.py:400
  (6 shorter events, 0.1 us)
Async XLA Ops:
  7.0 21.9 %all-to-all-start = ((bf16[16,4,16,256]{3,2,1,0:T(8,128)(2,1)}), bf16[16,4,16,256]{3,2,1,0:T(8,128)(2,1)S(1)}, u32[]{:S(2)}, u32[]{:S(2)}) async-start(bf16[16,4,16,256]{3,2,1,0:T(8,128)(2,1)} %get-tuple-element.13), calls=%async_computation | async-start | bytes 1048576 | tf_op jit(solution)/shard_map/all_to_all | solution.py:461
  14.4 14.6 %copy-start.2 = (bf16[128,256]{1,0:T(8,128)(2,1)S(1)}, bf16[128,256]{1,0:T(8,128)(2,1)}, u32[]{:S(2)}) copy-start(bf16[128,256]{1,0:T(8,128)(2,1)} %constant.17.clone.table_ref) | copy-start | bytes 196612
  14.4 24.8 %copy-start.1 = (bf16[256,128]{1,0:T(8,128)(2,1)S(1)}, bf16[256,128]{1,0:T(8,128)(2,1)}, u32[]{:S(2)}) copy-start(bf16[256,128]{1,0:T(8,128)(2,1)} %constant.18.clone.table_ref) | copy-start | bytes 196612
  21.6 34.0 %copy-start.8 = (bf16[64,64]{1,0:T(8,128)(2,1)S(1)}, bf16[64,64]{1,0:T(8,128)(2,1)}, u32[]{:S(2)}) copy-start(bf16[64,64]{1,0:T(8,128)(2,1)} %param.12) | copy-start | bytes 24580
  21.6 34.1 %copy-start.6 = (bf16[64,256]{1,0:T(8,128)(2,1)S(1)}, bf16[64,256]{1,0:T(8,128)(2,1)}, u32[]{:S(2)}) copy-start(bf16[64,256]{1,0:T(8,128)(2,1)} %param.14) | copy-start | bytes 98308
  21.6 34.3 %copy-start.7 = (bf16[64,256]{1,0:T(8,128)(2,1)S(1)}, bf16[64,256]{1,0:T(8,128)(2,1)}, u32[]{:S(2)}) copy-start(bf16[64,256]{1,0:T(8,128)(2,1)} %param.15) | copy-start | bytes 98308
  21.6 50.8 %copy-start.9 = (f32[64]{0:T(128)S(1)}, f32[64]{0:T(128)}, u32[]{:S(2)}) copy-start(f32[64]{0:T(128)} %param.13) | copy-start | bytes 772
  21.6 50.9 %copy-start = (bf16[64,1024]{1,0:T(8,128)(2,1)S(1)}, bf16[64,1024]{1,0:T(8,128)(2,1)}, u32[]{:S(2)}) copy-start(bf16[64,1024]{1,0:T(8,128)(2,1)} %constant.16.clone.lon_ref) | copy-start | bytes 393220
  21.6 50.9 %copy-start.3 = (bf16[256,64]{0,1:T(8,128)(2,1)S(1)}, bf16[256,64]{0,1:T(8,128)(2,1)}, u32[]{:S(2)}) copy-start(bf16[256,64]{0,1:T(8,128)(2,1)} %param.16) | copy-start | bytes 98308
  21.6 50.9 %copy-start.5 = (f32[4,16,128]{2,1,0:T(8,128)S(1)}, f32[4,16,128]{2,1,0:T(8,128)}, u32[]{:S(2)}) copy-start(f32[4,16,128]{2,1,0:T(8,128)} %get-tuple-element.20.loud_ref) | copy-start | bytes 98308
  29.2 20.5 %all-to-all-start.1 = ((bf16[16,4,16,256]{3,2,1,0:T(8,128)(2,1)}), bf16[16,4,16,256]{3,2,1,0:T(8,128)(2,1)S(1)}, u32[]{:S(2)}, u32[]{:S(2)}) async-start(bf16[16,4,16,256]{3,2,1,0:T(8,128)(2,1)} %get-tuple-element.16), calls=%async_computation.1 | async-start | bytes 1048576 | tf_op jit(solution)/shard_map/all_to_all | solution.py:461
  35.2 4.0 %collective-permute-start.1 = (bf16[1,64,256]{2,1,0:T(8,128)(2,1)S(1)}, bf16[1,64,256]{2,1,0:T(8,128)(2,1)S(1)}, u32[]{:S(2)}, u32[]{:S(2)}) collective-permute-start(bf16[1,64,256]{2,1,0:T(8,128)(2,1)S(1)} %slice_select_fusion.1), channel_id=1, source_target_pairs={{0,1},{1,0},{2,3},{3,2},{4,5},{5,4},{6,7},{7,6},{8,9},{9,8},{10,11... | collective-permute-start | bytes 98312 | tf_op jit(solution)/shard_map/ppermute | solution.py:427
  49.7 18.6 %all-to-all-start.3 = ((bf16[16,4,16,256]{3,2,1,0:T(8,128)(2,1)}), bf16[16,4,16,256]{3,2,1,0:T(8,128)(2,1)S(1)}, u32[]{:S(2)}, u32[]{:S(2)}) async-start(bf16[16,4,16,256]{3,2,1,0:T(8,128)(2,1)} %shard_map.106), calls=%async_computation.3 | async-start | bytes 1048576 | tf_op jit(solution)/shard_map/all_to_all | solution.py:469
  54.0 4.0 %collective-permute-start = (bf16[1,64,256]{2,1,0:T(8,128)(2,1)S(1)}, bf16[1,64,256]{2,1,0:T(8,128)(2,1)S(1)}, u32[]{:S(2)}, u32[]{:S(2)}) collective-permute-start(bf16[1,64,256]{2,1,0:T(8,128)(2,1)S(1)} %slice_select_fusion), channel_id=1, source_target_pairs={{0,1},{1,0},{2,3},{3,2},{4,5},{5,4},{6,7},{7,6},{8,9},{9,8},{10,11... | collective-permute-start | bytes 98312 | tf_op jit(solution)/shard_map/ppermute | solution.py:427
  68.3 31.0 %all-to-all-start.2 = ((bf16[16,4,16,256]{3,2,1,0:T(8,128)(2,1)}), bf16[16,4,16,256]{3,2,1,0:T(8,128)(2,1)S(1)}, u32[]{:S(2)}, u32[]{:S(2)}) async-start(bf16[16,4,16,256]{3,2,1,0:T(8,128)(2,1)} %shard_map.105), calls=%async_computation.2 | async-start | bytes 1048576 | tf_op jit(solution)/shard_map/all_to_all | solution.py:469
  72.5 26.7 %copy-start.4 = (f32[4,16,128]{2,1,0:T(8,128)S(1)}, f32[4,16,128]{2,1,0:T(8,128)}, u32[]{:S(2)}) copy-start(f32[4,16,128]{2,1,0:T(8,128)} %get-tuple-element.18.loud_ref) | copy-start | bytes 98308

commit v6 on v5

--- a/solution.py
+++ b/solution.py
@@ -462,8 +462,6 @@
         if b == 0:
             along, weight = lax.optimization_barrier((along, weight))
         modes = to_modes(gather_table, along)
-        if b + 1 < batch:
-            modes, sent[b + 1] = lax.optimization_barrier((modes, sent[b + 1]))
         below, above = neighbours(modes, sides)
         back = mix(below, modes, above, weight, spread_table, ranks)
         backs.append(lax.all_to_all(back, "rows", 0, 0, tiled=True))

time: 127 us -> 128 us (level)
  waiting for transfers between devices: 15.1 us -> 17 us
    all_to_all x2, waiting for transfers between devices: 5.44 us -> 7.38 us  [body(): along = lax.all_to_all(sent[b], 'rows', 0, 0, tiled=True)]
    all_to_all x2, starting transfers between devices: 13.4 us -> 11.5 us  [body(): along = lax.all_to_all(sent[b], 'rows', 0, 0, tiled=True)]
    all_to_all x2, starting transfers between devices: 8.2 us -> 10.1 us  [body(): backs.append(lax.all_to_all(back, 'rows', 0, 0, tiled=True))]
  transfers between devices with their start and end apart: 6 -> 6, of which waited for: 4 -> 4; matrix products, arithmetic and copies ran while one was open for 0% -> 0% of each run, Pallas kernels for 41% -> 40%
where the time goes in v6:
time: 128 us
  Pallas kernels  85.1 us (66%)
  starting transfers between devices  24.7 us (19%)
  waiting for transfers between devices  17 us (13%)
    pallas_call x2, Pallas kernels, finish(): call(functools.partial(finish_kernel, batch_at, ahead, reach), (1,), in_s...  53.4 us
    pallas_call x2, Pallas kernels, forward(): call(functools.partial(forward_kernel, ranks), (levels,), [pl.BlockSpec((...  14 us
    all_to_all x2, starting transfers between devices, body(): along = lax.all_to_all(sent[b], 'rows', 0, 0, tiled=True)  11.5 us
    all_to_all x2, starting transfers between devices, body(): backs.append(lax.all_to_all(back, 'rows', 0, 0, tiled=True))  10.1 us
    pallas_call x2, Pallas kernels, mix(): call(mix_kernel, (1,), [whole(below.shape), whole(modes.shape), whole(abo...  10 us
    all_to_all x2, waiting for transfers between devices, body(): along = lax.all_to_all(sent[b], 'rows', 0, 0, tiled=True)  7.38 us
    pallas_call x1, Pallas kernels, arrange(): call(arrange_kernel, (lat_modes // part,), [pl.BlockSpec((shifts, part, b...  7.21 us
    all_to_all x2, waiting for transfers between devices, body(): backs.append(lax.all_to_all(back, 'rows', 0, 0, tiled=True))  5.21 us
  transfers between devices with their start and end apart: 6, of which 4 were waited for; matrix products, arithmetic and copies ran while one was open for 0% of the time, Pallas kernels for 40%

profile of v6, /device:TPU:0, one launch (start us, length us, event | category | flops | bytes accessed | tf_op | source)
XLA Modules:
  0.0 127.7 jit_solution(3451135207997636052)
XLA Ops:
  0.0 7.0 %shard_map.102 = (bf16[16,4,16,256]{3,2,1,0:T(8,128)(2,1)}, f32[4,16,128]{2,1,0:T(8,128)}) custom-call(bf16[2,4,16,64,1024]{4,3,2,1,0:T(8,128)(2,1)} %field_ref.7, bf16[64,1024]{1,0:T(8,128)(2,1)} %constant.16.clone.lon_ref), custom_call_target="tpu_custom_call" | custom-call | flops 536870912 | bytes 8388608 | tf_op jit(solution)/shard_map/pallas_call | solution.py:105
  7.0 7.4 %all-to-all-start.1 = ((bf16[16,4,16,256]{3,2,1,0:T(8,128)(2,1)}), bf16[16,4,16,256]{3,2,1,0:T(8,128)(2,1)S(1)}, u32[]{:S(2)}, u32[]{:S(2)}) async-start(bf16[16,4,16,256]{3,2,1,0:T(8,128)(2,1)} %get-tuple-element.12), calls=%async_computation.1 | async-start | bytes 1048576 | tf_op jit(solution)/shard_map/all_to_all | solution.py:461
  14.4 0.0 copy-start.2
  14.4 0.0 copy-start.1
  14.4 7.0 %shard_map.100 = (bf16[16,4,16,256]{3,2,1,0:T(8,128)(2,1)}, f32[4,16,128]{2,1,0:T(8,128)}) custom-call(bf16[2,4,16,64,1024]{4,3,2,1,0:T(8,128)(2,1)} %field_ref.7, bf16[64,1024]{1,0:T(8,128)(2,1)} %constant.16.clone.lon_ref), custom_call_target="tpu_custom_call" | custom-call | flops 536870912 | bytes 8388608 | tf_op jit(solution)/shard_map/pallas_call | solution.py:105
  21.4 0.0 copy-start.8
  21.4 0.0 copy-start.6
  21.4 0.0 copy-start.7
  21.4 7.4 %all-to-all-done.1.along_ref = bf16[16,4,16,256]{3,2,1,0:T(8,128)(2,1)S(1)} async-done(((bf16[16,4,16,256]{3,2,1,0:T(8,128)(2,1)}), bf16[16,4,16,256]{3,2,1,0:T(8,128)(2,1)S(1)}, u32[]{:S(2)}, u32[]{:S(2)}) %all-to-all-start.1) | async-done | bytes 524320 | tf_op jit(solution)/shard_map/all_to_all | solution.py:461
  28.8 4.1 %all-to-all-start = ((bf16[16,4,16,256]{3,2,1,0:T(8,128)(2,1)}), bf16[16,4,16,256]{3,2,1,0:T(8,128)(2,1)S(1)}, u32[]{:S(2)}, u32[]{:S(2)}) async-start(bf16[16,4,16,256]{3,2,1,0:T(8,128)(2,1)} %get-tuple-element.11), calls=%async_computation | async-start | bytes 1048576 | tf_op jit(solution)/shard_map/all_to_all | solution.py:461
  32.9 0.0 copy-start.9
  32.9 0.0 copy-start
  33.0 0.0 copy-start.3
  33.0 0.0 copy-start.5
  33.0 7.2 %shard_map.103.weight_ref = bf16[64,192,256]{2,1,0:T(8,128)(2,1)} custom-call(bf16[3,64,4,64,64]{4,3,2,1,0:T(8,128)(2,1)} %weight_ref.1), custom_call_target="tpu_custom_call" | custom-call | flops 3145728 | bytes 18874368 | tf_op jit(solution)/shard_map/pallas_call | solution.py:166
  40.2 0.0 copy-done.2
  40.2 0.2 shard_map.105.modes_ref
  40.4 1.6 %collective-permute-start.1 = (bf16[1,64,256]{2,1,0:T(8,128)(2,1)S(1)}, bf16[1,64,256]{2,1,0:T(8,128)(2,1)S(1)}, u32[]{:S(2)}, u32[]{:S(2)}) collective-permute-start(bf16[1,64,256]{2,1,0:T(8,128)(2,1)S(1)} %slice_select_fusion), channel_id=1, source_target_pairs={{0,1},{1,0},{2,3},{3,2},{4,5},{5,4},{6,7},{7,6},{8,9},{9,8},{10,11... | collective-permute-start | bytes 98312 | tf_op jit(solution)/shard_map/ppermute | solution.py:427
  42.0 2.4 %collective-permute-done.1 = bf16[1,64,256]{2,1,0:T(8,128)(2,1)S(1)} collective-permute-done((bf16[1,64,256]{2,1,0:T(8,128)(2,1)S(1)}, bf16[1,64,256]{2,1,0:T(8,128)(2,1)S(1)}, u32[]{:S(2)}, u32[]{:S(2)}) %collective-permute-start.1) | collective-permute-done | bytes 32800 | tf_op jit(solution)/shard_map/ppermute | solution.py:427
  44.4 0.0 copy-done.1
  44.4 5.0 %shard_map.106 = bf16[16,4,16,256]{3,2,1,0:T(8,128)(2,1)} custom-call(bf16[1,64,256]{2,1,0:T(8,128)(2,1)S(1)} %get-tuple-element.18.below_ref, bf16[4,64,256]{2,1,0:T(8,128)(2,1)S(1)} %shard_map.105.modes_ref, bf16[1,64,256]{2,1,0:T(8,128)(2,1)S(1)} %get-tuple-element.17.above_ref, bf16[64,192,256]{2,1,0:T(8,128)(2,1)} %shard_map.103.weight_ref, ...), custom_call_target="tpu_custom_call" | custom-call | flops 25165824 | bytes 6291456 | tf_op jit(solution)/shard_map/pallas_call | solution.py:218
  49.4 0.0 all-to-all-done.along_ref
  49.4 6.0 %all-to-all-start.3 = ((bf16[16,4,16,256]{3,2,1,0:T(8,128)(2,1)}), bf16[16,4,16,256]{3,2,1,0:T(8,128)(2,1)S(1)}, u32[]{:S(2)}, u32[]{:S(2)}) async-start(bf16[16,4,16,256]{3,2,1,0:T(8,128)(2,1)} %shard_map.106), calls=%async_computation.3 | async-start | bytes 1048576 | tf_op jit(solution)/shard_map/all_to_all | solution.py:467
  55.5 0.2 shard_map.101.modes_ref
  55.7 1.6 %collective-permute-start = (bf16[1,64,256]{2,1,0:T(8,128)(2,1)S(1)}, bf16[1,64,256]{2,1,0:T(8,128)(2,1)S(1)}, u32[]{:S(2)}, u32[]{:S(2)}) collective-permute-start(bf16[1,64,256]{2,1,0:T(8,128)(2,1)S(1)} %slice_select_fusion.1), channel_id=1, source_target_pairs={{0,1},{1,0},{2,3},{3,2},{4,5},{5,4},{6,7},{7,6},{8,9},{9,8},{10,11... | collective-permute-start | bytes 98312 | tf_op jit(solution)/shard_map/ppermute | solution.py:427
  57.3 0.0 copy-done.8
  57.3 0.1 copy.15
  57.4 0.0 copy-done.6
  57.4 0.1 copy.16
  57.5 0.0 copy-done.7
  57.5 0.1 copy.18
  57.6 2.0 %collective-permute-done = bf16[1,64,256]{2,1,0:T(8,128)(2,1)S(1)} collective-permute-done((bf16[1,64,256]{2,1,0:T(8,128)(2,1)S(1)}, bf16[1,64,256]{2,1,0:T(8,128)(2,1)S(1)}, u32[]{:S(2)}, u32[]{:S(2)}) %collective-permute-start) | collective-permute-done | bytes 32800 | tf_op jit(solution)/shard_map/ppermute | solution.py:427
  59.7 5.0 %shard_map.104 = bf16[16,4,16,256]{3,2,1,0:T(8,128)(2,1)} custom-call(bf16[1,64,256]{2,1,0:T(8,128)(2,1)S(1)} %get-tuple-element.20.below_ref, bf16[4,64,256]{2,1,0:T(8,128)(2,1)S(1)} %shard_map.101.modes_ref, bf16[1,64,256]{2,1,0:T(8,128)(2,1)S(1)} %get-tuple-element.19.above_ref, bf16[64,192,256]{2,1,0:T(8,128)(2,1)} %shard_map.103.weight_ref, ...), custom_call_target="tpu_custom_call" | custom-call | flops 25165824 | bytes 6291456 | tf_op jit(solution)/shard_map/pallas_call | solution.py:218
  64.7 5.2 %all-to-all-done.3.back_ref = bf16[16,4,16,256]{3,2,1,0:T(8,128)(2,1)S(1)} async-done(((bf16[16,4,16,256]{3,2,1,0:T(8,128)(2,1)}), bf16[16,4,16,256]{3,2,1,0:T(8,128)(2,1)S(1)}, u32[]{:S(2)}, u32[]{:S(2)}) %all-to-all-start.3) | async-done | bytes 524320 | tf_op jit(solution)/shard_map/all_to_all | solution.py:467
  69.9 4.1 %all-to-all-start.2 = ((bf16[16,4,16,256]{3,2,1,0:T(8,128)(2,1)}), bf16[16,4,16,256]{3,2,1,0:T(8,128)(2,1)S(1)}, u32[]{:S(2)}, u32[]{:S(2)}) async-start(bf16[16,4,16,256]{3,2,1,0:T(8,128)(2,1)} %shard_map.104), calls=%async_computation.2 | async-start | bytes 1048576 | tf_op jit(solution)/shard_map/all_to_all | solution.py:467
  74.1 0.0 copy-done.9
  74.1 0.1 broadcast_in_dim.2.bias_ref
  74.2 0.0 copy-done
  74.2 0.0 copy-done.3
  74.2 0.0 copy-done.5
  74.2 0.0 copy-start.4
  74.2 26.7 %shard_map.107.rest_0_ = bf16[2,4,16,64,1024]{4,3,2,1,0:T(8,128)(2,1)} custom-call(bf16[16,4,16,256]{3,2,1,0:T(8,128)(2,1)S(1)} %all-to-all-done.3.back_ref, bf16[64,1024]{1,0:T(8,128)(2,1)S(1)} %copy-done, bf16[64,64]{1,0:T(8,128)(2,1)S(1)} %bitcast.4, f32[64,256]{1,0:T(8,128)S(1)} %broadcast_in_dim.2.bias_ref, ...), custom_call_target="tpu_custom_call" | custom-call | flops 7516192768 | bytes 16777216 | tf_op jit(solution)/shard_map/pallas_call | solution.py:400
  100.9 0.0 all-to-all-done.2.back_ref
  100.9 0.0 copy-done.4
  100.9 26.7 %shard_map.108 = bf16[2,4,16,64,1024]{4,3,2,1,0:T(8,128)(2,1)} custom-call(bf16[16,4,16,256]{3,2,1,0:T(8,128)(2,1)S(1)} %all-to-all-done.2.back_ref, bf16[64,1024]{1,0:T(8,128)(2,1)S(1)} %copy-done, bf16[64,64]{1,0:T(8,128)(2,1)S(1)} %bitcast.5, f32[64,256]{1,0:T(8,128)S(1)} %broadcast_in_dim.2.bias_ref, ...), custom_call_target="tpu_custom_call", output_to_operand_aliasing={{}: (8, {})} | custom-call | flops 7516192768 | bytes 16777216 | tf_op jit(solution)/shard_map/pallas_call | solution.py:400
  (6 shorter events, 0.1 us)
Async XLA Ops:
  7.0 21.8 %all-to-all-start.1 = ((bf16[16,4,16,256]{3,2,1,0:T(8,128)(2,1)}), bf16[16,4,16,256]{3,2,1,0:T(8,128)(2,1)S(1)}, u32[]{:S(2)}, u32[]{:S(2)}) async-start(bf16[16,4,16,256]{3,2,1,0:T(8,128)(2,1)} %get-tuple-element.12), calls=%async_computation.1 | async-start | bytes 1048576 | tf_op jit(solution)/shard_map/all_to_all | solution.py:461
  14.4 25.8 %copy-start.2 = (bf16[128,256]{1,0:T(8,128)(2,1)S(1)}, bf16[128,256]{1,0:T(8,128)(2,1)}, u32[]{:S(2)}) copy-start(bf16[128,256]{1,0:T(8,128)(2,1)} %constant.17.clone.table_ref) | copy-start | bytes 196612
  14.4 30.1 %copy-start.1 = (bf16[256,128]{1,0:T(8,128)(2,1)S(1)}, bf16[256,128]{1,0:T(8,128)(2,1)}, u32[]{:S(2)}) copy-start(bf16[256,128]{1,0:T(8,128)(2,1)} %constant.18.clone.table_ref) | copy-start | bytes 196612
  21.4 35.9 %copy-start.8 = (bf16[64,64]{1,0:T(8,128)(2,1)S(1)}, bf16[64,64]{1,0:T(8,128)(2,1)}, u32[]{:S(2)}) copy-start(bf16[64,64]{1,0:T(8,128)(2,1)} %param.12) | copy-start | bytes 24580
  21.4 36.0 %copy-start.6 = (bf16[64,256]{1,0:T(8,128)(2,1)S(1)}, bf16[64,256]{1,0:T(8,128)(2,1)}, u32[]{:S(2)}) copy-start(bf16[64,256]{1,0:T(8,128)(2,1)} %param.14) | copy-start | bytes 98308
  21.4 36.1 %copy-start.7 = (bf16[64,256]{1,0:T(8,128)(2,1)S(1)}, bf16[64,256]{1,0:T(8,128)(2,1)}, u32[]{:S(2)}) copy-start(bf16[64,256]{1,0:T(8,128)(2,1)} %param.15) | copy-start | bytes 98308
  28.8 20.6 %all-to-all-start = ((bf16[16,4,16,256]{3,2,1,0:T(8,128)(2,1)}), bf16[16,4,16,256]{3,2,1,0:T(8,128)(2,1)S(1)}, u32[]{:S(2)}, u32[]{:S(2)}) async-start(bf16[16,4,16,256]{3,2,1,0:T(8,128)(2,1)} %get-tuple-element.11), calls=%async_computation | async-start | bytes 1048576 | tf_op jit(solution)/shard_map/all_to_all | solution.py:461
  32.9 41.2 %copy-start.9 = (f32[64]{0:T(128)S(1)}, f32[64]{0:T(128)}, u32[]{:S(2)}) copy-start(f32[64]{0:T(128)} %param.13) | copy-start | bytes 772
  32.9 41.2 %copy-start = (bf16[64,1024]{1,0:T(8,128)(2,1)S(1)}, bf16[64,1024]{1,0:T(8,128)(2,1)}, u32[]{:S(2)}) copy-start(bf16[64,1024]{1,0:T(8,128)(2,1)} %constant.16.clone.lon_ref) | copy-start | bytes 393220
  33.0 41.2 %copy-start.3 = (bf16[256,64]{0,1:T(8,128)(2,1)S(1)}, bf16[256,64]{0,1:T(8,128)(2,1)}, u32[]{:S(2)}) copy-start(bf16[256,64]{0,1:T(8,128)(2,1)} %param.16) | copy-start | bytes 98308
  33.0 41.2 %copy-start.5 = (f32[4,16,128]{2,1,0:T(8,128)S(1)}, f32[4,16,128]{2,1,0:T(8,128)}, u32[]{:S(2)}) copy-start(f32[4,16,128]{2,1,0:T(8,128)} %get-tuple-element.16.loud_ref) | copy-start | bytes 98308
  40.4 4.0 %collective-permute-start.1 = (bf16[1,64,256]{2,1,0:T(8,128)(2,1)S(1)}, bf16[1,64,256]{2,1,0:T(8,128)(2,1)S(1)}, u32[]{:S(2)}, u32[]{:S(2)}) collective-permute-start(bf16[1,64,256]{2,1,0:T(8,128)(2,1)S(1)} %slice_select_fusion), channel_id=1, source_target_pairs={{0,1},{1,0},{2,3},{3,2},{4,5},{5,4},{6,7},{7,6},{8,9},{9,8},{10,11... | collective-permute-start | bytes 98312 | tf_op jit(solution)/shard_map/ppermute | solution.py:427
  49.4 20.5 %all-to-all-start.3 = ((bf16[16,4,16,256]{3,2,1,0:T(8,128)(2,1)}), bf16[16,4,16,256]{3,2,1,0:T(8,128)(2,1)S(1)}, u32[]{:S(2)}, u32[]{:S(2)}) async-start(bf16[16,4,16,256]{3,2,1,0:T(8,128)(2,1)} %shard_map.106), calls=%async_computation.3 | async-start | bytes 1048576 | tf_op jit(solution)/shard_map/all_to_all | solution.py:467
  55.7 4.0 %collective-permute-start = (bf16[1,64,256]{2,1,0:T(8,128)(2,1)S(1)}, bf16[1,64,256]{2,1,0:T(8,128)(2,1)S(1)}, u32[]{:S(2)}, u32[]{:S(2)}) collective-permute-start(bf16[1,64,256]{2,1,0:T(8,128)(2,1)S(1)} %slice_select_fusion.1), channel_id=1, source_target_pairs={{0,1},{1,0},{2,3},{3,2},{4,5},{5,4},{6,7},{7,6},{8,9},{9,8},{10,11... | collective-permute-start | bytes 98312 | tf_op jit(solution)/shard_map/ppermute | solution.py:427
  69.9 31.0 %all-to-all-start.2 = ((bf16[16,4,16,256]{3,2,1,0:T(8,128)(2,1)}), bf16[16,4,16,256]{3,2,1,0:T(8,128)(2,1)S(1)}, u32[]{:S(2)}, u32[]{:S(2)}) async-start(bf16[16,4,16,256]{3,2,1,0:T(8,128)(2,1)} %shard_map.104), calls=%async_computation.2 | async-start | bytes 1048576 | tf_op jit(solution)/shard_map/all_to_all | solution.py:467
  74.2 26.7 %copy-start.4 = (f32[4,16,128]{2,1,0:T(8,128)S(1)}, f32[4,16,128]{2,1,0:T(8,128)}, u32[]{:S(2)}) copy-start(f32[4,16,128]{2,1,0:T(8,128)} %get-tuple-element.14.loud_ref) | copy-start | bytes 98308
